TPU v7x, 32 devices: a whole 2x2x4 slice. The times are simulated.
32 devices in a mesh: chan: 32 (over z, y, x, core), win: 1.
Axes of the slice: x: 2, y: 2, z: 4, core: 2. Of those that a mesh axis runs over, the one named last changes fastest.
Arguments:
- traces: bfloat16 [512, 48, 1500], P('chan', 'win'), may hold values from -6 to 6
- source_index: int32 [64], replicated, may hold values from 0 to 511
Outputs:
- stack: float32 [2, 64, 512, 256], P(None, 'win', 'chan')
All inputs are finite; a program needn't handle non-finite values.
Results may differ from a plain program's by a relative error of at most 0.0058.
Values may be sent and summed in bfloat16 or wider, within the bound.
No kernel may reach another device: no remote copies, remote signals or barrier semaphores. Data moves between devices by JAX's collectives and lax.ppermute only.
A program may use at most 64 MiB of HBM per device.

v0:
```python
import functools
import math

import jax
import jax.numpy as jnp
import ml_dtypes
import numpy as np
from jax import lax
from jax.experimental import pallas as pl
from jax.experimental.pallas import tpu as pltpu
from jax.sharding import PartitionSpec as P

F = 256
HALF = 128
F0 = 1
K = 64
GAUGE = 4
LANES = 128
PITCH = F + 8
HALF_PITCH = HALF + 8
VMEM_LIMIT = 24 * 1024 * 1024


def make_table(length):
    times = np.arange(length, dtype=np.int64)[:, None]
    bins = np.arange(F, dtype=np.int64)[None, :] + F0
    phase = (times * bins % length).astype(np.float32) * np.float32(2.0 * math.pi / length)
    phase = phase.astype(np.float64)
    return np.concatenate([np.cos(phase), -np.sin(phase)], axis=1).astype(ml_dtypes.bfloat16)


def make_band():
    rows = np.arange(F)[:, None]
    cols = np.arange(F)[None, :]
    return (np.abs(rows - cols) <= K).astype(ml_dtypes.bfloat16)


def whiten_block(cur, upper, table_ref, band_ref, turned_ref, first):
    chans, wins, length = cur.shape
    rows = chans * wins
    diff = (upper.astype(jnp.float32) - cur.astype(jnp.float32)).reshape(rows, length)
    power = jnp.sum(diff * diff, axis=1, keepdims=True) * (1.0 / length)
    normed = (diff * lax.rsqrt(power + 1e-05)).astype(jnp.bfloat16)
    spec = jnp.dot(normed, table_ref[...], preferred_element_type=jnp.float32)
    real = spec[:, :F]
    imag = spec[:, F:]
    magnitude = jnp.sqrt(real * real + imag * imag).astype(jnp.bfloat16)
    bins = lax.broadcasted_iota(jnp.int32, (1, F), 1)
    counts = (jnp.minimum(bins, K) + jnp.minimum(F - 1 - bins, K) + 1).astype(jnp.float32)
    smooth = jnp.dot(magnitude, band_ref[...], preferred_element_type=jnp.float32) / counts
    gain = 1.0 / (smooth + 1e-06)
    white_re = (real * gain).astype(jnp.bfloat16).astype(jnp.float32)
    white_im = (imag * gain).astype(jnp.bfloat16).astype(jnp.float32)
    pad = jnp.zeros((LANES - 2 * wins, F), jnp.float32)
    for c in range(chans):
        mine = slice(c * wins, (c + 1) * wins)
        both = jnp.concatenate([white_re[mine], white_im[mine], pad], axis=0)
        turned_ref[(first + c) * PITCH : (first + c) * PITCH + F, :] = both.T


def list_slots(chans, me_ref, index_ref, slot_ref):
    mine = jnp.int32(0)
    for s in range(index_ref.shape[0]):
        local = index_ref[s] - me_ref[0] * chans
        bit = lax.shift_left(jnp.int32(1), jnp.clip(local, 0, chans - 1))
        mine = mine | jnp.where((local >= 0) & (local < chans), bit, 0)
    early = count = jnp.int32(0)
    for c in range(chans):
        slot_ref[count] = c
        count = count + (lax.shift_right_logical(mine, c) & 1)
        if c < chans - GAUGE:
            early = count
    slot_ref[chans + 1] = early
    slot_ref[chans + 2] = count


def lay_out(slot, channel, turned_ref, stage_ref, height, slots):
    dests = stage_ref.shape[1] // height
    per_dest = HALF // dests
    lane = lax.broadcasted_iota(jnp.int32, (dests, LANES), 1)
    for pair in range(per_dest // 2):
        piece = []
        for j in range(2):
            for half in range(2):
                at = channel * PITCH + half * HALF + pair * 2 + j
                piece.append(turned_ref[pl.ds(at, dests, stride=per_dest), :])
        a, b, c, d = piece
        b = pltpu.roll(b, 96, 1)
        c = pltpu.roll(c, 64, 1)
        d = pltpu.roll(d, 32, 1)
        rows_at = pl.ds(pair * slots + slot, dests, stride=height)
        stage_ref.at[0][rows_at, :] = jnp.where(lane < 96, a, b)
        stage_ref.at[1][rows_at, :] = jnp.where(lane < 64, b, c)
        stage_ref.at[2][rows_at, :] = jnp.where(lane < 32, c, d)


def whiten_kernel(
    height, slots, me_ref, index_ref, traces_ref, table_ref, band_ref, turned_ref, stage_ref, slot_ref
):
    chans = traces_ref.shape[0]
    stage_ref[...] = jnp.zeros_like(stage_ref)
    list_slots(chans, me_ref, index_ref, slot_ref)
    for c in range(0, chans - GAUGE, GAUGE):
        cur, upper = traces_ref[c : c + GAUGE], traces_ref[c + GAUGE : c + 2 * GAUGE]
        whiten_block(cur, upper, table_ref, band_ref, turned_ref, c)

    def one(slot, carry):
        lay_out(slot, slot_ref[slot], turned_ref, stage_ref, height, slots)
        return carry

    lax.fori_loop(0, jnp.minimum(slot_ref[chans + 1], slots), one, 0)


def finish_kernel(
    height, slots, slot_ref, traces_ref, halo_ref, table_ref, band_ref, _, __, turned_ref, stage_ref, *rounds
):
    chans = traces_ref.shape[0]
    early, count = slot_ref[chans + 1], slot_ref[chans + 2]
    cur = traces_ref[chans - GAUGE :]
    whiten_block(cur, halo_ref[...], table_ref, band_ref, turned_ref, chans - GAUGE)

    def fill(first, start, rows_ref):
        def one(slot, carry):
            channel = slot_ref[first + slot]
            lay_out(slot, channel, turned_ref, stage_ref, height, slots)
            return carry

        lax.fori_loop(start, jnp.minimum(count - first, slots), one, 0)
        for dest in range(rows_ref.shape[0]):
            for tile in range(3):
                block = stage_ref[tile, dest * height : (dest + 1) * height, :]
                rows_ref[dest, :, tile * LANES : (tile + 1) * LANES] = block.astype(jnp.bfloat16)

    def clear(rows_ref):
        rows_ref[...] = jnp.zeros_like(rows_ref)

    fill(0, early, rounds[0])
    for number in range(1, len(rounds)):
        more = count > number * slots
        pl.when(more)(functools.partial(fill, number * slots, 0, rounds[number]))
        pl.when(jnp.logical_not(more))(functools.partial(clear, rounds[number]))


def left_kernel(chans, depth, turned_ref, left_ref):
    lane = lax.broadcasted_iota(jnp.int32, (chans, LANES), 1)

    def one(g, carry):
        stack = []
        for half in range(2):
            real = turned_ref[pl.ds(half * HALF + g, chans, stride=PITCH), :]
            ahead = pltpu.roll(real, depth // 2, 1)
            back = pltpu.roll(real, LANES - depth // 2, 1)
            stack += [real, jnp.where(lane < depth // 2, -back, ahead)]
        left_ref[g] = jnp.concatenate(stack, axis=0).astype(jnp.bfloat16)
        return carry

    lax.fori_loop(0, HALF, one, 0, unroll=8)


def pick_kernel(slots, base, place_ref, rows_ref, out_ref):
    sources = place_ref.shape[0]
    dests, height, width = rows_ref.shape
    groups, depth, _ = out_ref.shape
    rows = rows_ref[...].reshape(dests * height, width)
    ids = lax.broadcasted_iota(jnp.int32, (sources, dests * height), 1)
    place = place_ref[...] - base
    inside = (place >= 0) & (place < dests * slots)
    spot = place // slots * height + place % slots
    for pair in range(groups // 2):
        hit = inside & (ids == spot + pair * slots)
        onehot = jnp.where(hit, 1.0, 0.0).astype(jnp.bfloat16)
        turned = jnp.dot(onehot, rows, preferred_element_type=jnp.float32).T
        for j in range(2):
            low = turned[(2 * j) * depth : (2 * j + 1) * depth]
            high = turned[(2 * j + 1) * depth : (2 * j + 2) * depth]
            out_ref[pair * 2 + j] = jnp.concatenate([low, high], axis=1).astype(jnp.bfloat16)


def products(n, origins, me_ref, left_ref, pieces, held):
    rows = left_ref.shape[1]
    depth, width = pieces[0].shape[-2:]
    groups = HALF // n
    sources = width // 2
    outs = rows // 2
    me = me_ref[0]
    lane = lax.broadcasted_iota(jnp.int32, (outs, width), 1)
    for piece, names in zip(pieces, origins):
        for place, (flip, index) in enumerate(names):
            g = (me ^ flip) * groups + index
            both = jnp.dot(left_ref[g][:, :depth], piece[place], preferred_element_type=jnp.float32)
            mine = jnp.where(lane < sources, both[:outs], both[outs:])
            held[pl.ds(g, outs, stride=HALF_PITCH), :] = mine


def partial_kernel(n, origins, chained, me_ref, left_ref, *refs):
    products(n, origins, me_ref, left_ref, refs[chained:-1], refs[-1])


def correlate_kernel(scale, n, origins, sources, me_ref, left_ref, _, *refs):
    pieces, (out_ref, held, turned_ref, sems) = refs[:-4], refs[-4:]
    products(n, origins, me_ref, left_ref, pieces, held)
    outs = held.shape[0] // HALF_PITCH
    chans = outs // 2
    group = 8
    copies = []
    for part in range(2):
        for c in range(chans):
            base = (part * chans + c) * HALF_PITCH
            turned = held[base : base + HALF, :].T * scale
            rows_at = pl.ds(part * sources * chans + c, sources, stride=chans)
            for half in range(2):
                turned_ref.at[half][rows_at, :] = turned[half * sources : (half + 1) * sources]
            if c % group == group - 1:
                span = pl.ds(c + 1 - group, group)
                for half in range(2):
                    block = turned_ref.at[half].reshape(2, sources, chans, HALF)
                    copy = pltpu.make_async_copy(
                        block.at[part, :, span, :],
                        out_ref.at[part, :, span, pl.ds(half * HALF, HALF)],
                        sems.at[part * (chans // group) + c // group, half],
                    )
                    copy.start()
                    copies.append(copy)
    for copy in copies:
        copy.wait()


def gather_pieces(own, multiply, after_products):
    n = lax.axis_size("chan")
    groups = own.shape[0]
    core, x, y, z, zz = 1, 2, 4, 8, 16
    place = {}

    def keep(array, names):
        for i, name in enumerate(names):
            place[name] = (array, i)
        return array, names

    def pack(names):
        parts = []
        for name in names:
            array, i = place[name]
            if parts and parts[-1][0] is array and parts[-1][2] == i:
                parts[-1][2] = i + 1
            else:
                parts.append([array, i, i + 1])
        blocks = [array[i:j] for array, i, j in parts]
        return blocks[0] if len(blocks) == 1 else jnp.concatenate(blocks, axis=0)

    def send(names, flip):
        route = [(i, i ^ flip) for i in range(n)]
        return lax.ppermute(pack(names), "chan", route), [(f ^ flip, g) for f, g in names]

    def lists(pairs):
        return [array for array, _ in pairs], [names for _, names in pairs]

    def piece(flip):
        return [(flip, g) for g in range(groups)]

    near = [keep(own, piece(0))]
    if n != 32:
        flip = 1
        while flip < n:
            near.append(keep(*send(sorted(place), flip)))
            flip *= 2
        multiply(*lists(near[:-1]))
        return lists(near[-1:])

    first = [send(piece(0), flip) for flip in (x ^ y, y, x, z, zz)]
    arrays = lax.optimization_barrier(lists(first)[0])
    near += [keep(array, names) for array, (_, names) in zip(arrays, first)]
    mid = [
        send(piece(z) + piece(zz), x),
        send(piece(z) + piece(zz), y),
        send(piece(x ^ y), zz),
        send(piece(zz) + piece(x ^ y), z),
    ]
    multiply(*lists(near))
    arrays = after_products(*lists(mid)[0])
    mid = [keep(array, names) for array, (_, names) in zip(arrays, mid)]
    last = [
        send(piece(z ^ zz), x),
        send(piece(z ^ zz), y),
        send(piece(zz ^ x ^ y), z),
    ]
    theirs = send([name for pair in near + mid for name in pair[1]], core)
    multiply(*lists(mid))
    arrays = after_products(*lists(last)[0])
    last = [keep(array, names) for array, (_, names) in zip(arrays, last)]
    assert sorted(place) == [(f, g) for f in range(0, n, 2) for g in range(groups)]
    final = send([name for pair in last for name in pair[1]], core)
    multiply(*lists([theirs] + last))
    return lists([final])


def plan_places(source_index, chans, slots):
    n = lax.axis_size("chan")
    channels = jnp.arange(n * chans, dtype=jnp.int32)
    hits = source_index[:, None] == channels[None, :]
    listed = jnp.any(hits, axis=0).reshape(n, chans).astype(jnp.int32)
    below = (jnp.arange(chans)[:, None] < jnp.arange(chans)[None, :]).astype(jnp.int32)
    rank = jnp.sum(listed[:, :, None] * below[None], axis=1)
    device = jnp.arange(n, dtype=jnp.int32)[:, None]
    place = (rank // slots * n + device) * slots + rank % slots
    places = jnp.sum(jnp.where(hits, place.reshape(1, -1), 0), axis=1, keepdims=True)
    return places, jnp.max(jnp.sum(listed, axis=1))


def per_device(traces, source_index):
    chans, wins, length = traces.shape
    n = lax.axis_size("chan")
    sources = source_index.shape[0]
    halo = lax.ppermute(traces[:GAUGE], "chan", [(i + 1, i) for i in range(n - 1)])
    me = lax.axis_index("chan").astype(jnp.int32).reshape(1)
    table, band = jnp.asarray(make_table(length)), jnp.asarray(make_band())
    depth = 2 * wins
    row_width = HALF * 2 * depth // n
    vmem = pl.BlockSpec(memory_space=pltpu.VMEM)
    smem = pl.BlockSpec(memory_space=pltpu.SMEM)
    params = pltpu.CompilerParams(vmem_limit_bytes=VMEM_LIMIT)
    pairs = HALF // n // 2
    slots = chans // pairs
    turned = jax.ShapeDtypeStruct((chans * PITCH, LANES), jnp.float32)
    stage = jax.ShapeDtypeStruct((3, n * chans, LANES), jnp.float32)
    slot_list = jax.ShapeDtypeStruct((chans + 3,), jnp.int32)
    some, staged, listed = pl.pallas_call(
        functools.partial(whiten_kernel, chans, slots),
        in_specs=[smem] * 2 + [vmem] * 3,
        out_specs=[vmem, vmem, smem],
        out_shape=[turned, stage, slot_list],
        compiler_params=params,
        cost_estimate=pl.CostEstimate(
            flops=2 * (chans - GAUGE) * wins * (length + F // 2) * 2 * F,
            bytes_accessed=8 * 1024 * 1024,
            transcendentals=0,
        ),
        name="whiten",
    )(me, source_index, traces, table, band)
    rows_shape = jax.ShapeDtypeStruct((n, chans, row_width // pairs), jnp.bfloat16)
    spectra, _, *rounds = pl.pallas_call(
        functools.partial(finish_kernel, chans, slots),
        in_specs=[smem] + [vmem] * 6,
        out_specs=[vmem] * (2 + pairs),
        out_shape=[turned, stage] + [rows_shape] * pairs,
        input_output_aliases={5: 0, 6: 1},
        compiler_params=params,
        name="finish",
    )(listed, traces, halo, table, band, some, staged)
    rounds[0], late_index = lax.optimization_barrier((rounds[0], source_index))
    places, most = plan_places(late_index, chans, slots)

    def exchange(number, rows):
        rows = lax.all_to_all(rows, "chan", 0, 0, tiled=True)
        return pl.pallas_call(
            functools.partial(pick_kernel, slots, number * n * slots),
            out_shape=jax.ShapeDtypeStruct((HALF // n, depth, 2 * sources), jnp.bfloat16),
            compiler_params=params,
            name="pick",
        )(places, rows)

    picked = exchange(0, rounds[0])
    for number in range(1, pairs):
        picked = lax.cond(
            most > number * slots,
            lambda p, r, number=number: p + exchange(number, r),
            lambda p, r: p,
            picked,
            rounds[number],
        )
    picked, spectra = lax.optimization_barrier((picked, spectra))
    left = pl.pallas_call(
        functools.partial(left_kernel, chans, depth),
        in_specs=[vmem],
        out_specs=vmem,
        out_shape=jax.ShapeDtypeStruct((HALF, 4 * chans, LANES), jnp.bfloat16),
        compiler_params=params,
        cost_estimate=pl.CostEstimate(
            flops=10 * 1000 * 1000, bytes_accessed=8 * 1024 * 1024, transcendentals=0
        ),
        name="left",
    )(spectra)
    total_windows = wins * lax.axis_size("win")
    held_shape = jax.ShapeDtypeStruct((2 * chans * HALF_PITCH, LANES), jnp.float32)
    held = []

    def multiply(pieces, origins):
        held[:] = [
            pl.pallas_call(
                functools.partial(partial_kernel, n, origins, len(held)),
                in_specs=[smem, vmem] + [vmem] * (len(held) + len(pieces)),
                out_specs=vmem,
                out_shape=held_shape,
                input_output_aliases={2: 0} if held else {},
                compiler_params=params,
                cost_estimate=pl.CostEstimate(
                    flops=100 * 1000 * 1000, bytes_accessed=4 * 1024 * 1024, transcendentals=0
                ),
                name="products",
            )(me, left, *held, *pieces)
        ]

    def after_products(*arrays):
        *arrays, held[0] = lax.optimization_barrier((*arrays, held[0]))
        return arrays

    pieces, origins = gather_pieces(picked, multiply, after_products)
    stack, _ = pl.pallas_call(
        functools.partial(correlate_kernel, 1.0 / total_windows, n, origins, sources),
        in_specs=[smem, vmem, vmem] + [vmem] * len(pieces),
        out_specs=[pl.BlockSpec(memory_space=pl.ANY), vmem],
        out_shape=[jax.ShapeDtypeStruct((2, sources, chans, F), jnp.float32), held_shape],
        scratch_shapes=[
            pltpu.VMEM((2, 2 * sources * chans, HALF), jnp.float32),
            pltpu.SemaphoreType.DMA((chans // 4, 2)),
        ],
        input_output_aliases={2: 1},
        compiler_params=params,
        name="correlate",
    )(me, left, *held, *pieces)
    if lax.axis_size("win") == 1:
        return stack
    return lax.psum_scatter(stack, "win", scatter_dimension=1, tiled=True)


def solution(mesh):
    return jax.shard_map(
        per_device,
        mesh=mesh,
        in_specs=(P("chan", "win", None), P()),
        out_specs=P(None, "win", "chan", None),
        check_vma=False,
    )
```

profile of v0, /device:TPU:0, one launch (start us, length us, event | category | flops | bytes accessed | tf_op | source)
XLA Modules:
  0.0 65.1 jit_solution(4424696278274317982)
XLA Ops:
  0.0 1.1 %slice.7 = bf16[4,48,1500]{2,1,0:T(8,128)(2,1)S(1)} slice(bf16[16,48,1500]{2,1,0:T(8,128)(2,1)} %traces_ref.3), slice={[0:4], [0:48], [0:1500]} | slice | bytes 1152000 | tf_op jit(solution)/shard_map/slice | solution.py:313
  1.1 1.3 %collective-permute-start = (bf16[4,48,1500]{2,1,0:T(8,128)(2,1)S(1)}, bf16[4,48,1500]{2,1,0:T(8,128)(2,1)S(1)}, u32[]{:S(2)}, u32[]{:S(2)}) collective-permute-start(bf16[4,48,1500]{2,1,0:T(8,128)(2,1)S(1)} %slice.7), channel_id=1, source_target_pairs={{1,0},{2,1},{3,2},{4,3},{5,4},{6,5},{7,6},{8,7},{9,8},{10,9},{11,1... | collective-permute-start | bytes 1728008 | tf_op jit(solution)/shard_map/ppermute | solution.py:313
  2.5 1.7 %copy-done = bf16[16,48,1500]{2,1,0:T(8,128)(2,1)S(1)} copy-done((bf16[16,48,1500]{2,1,0:T(8,128)(2,1)S(1)}, bf16[16,48,1500]{2,1,0:T(8,128)(2,1)}, u32[]{:S(2)}) %copy-start) | copy-done | bytes 2304024
  4.1 1.4 %copy-done.2 = bf16[1500,512]{1,0:T(8,128)(2,1)S(1)} copy-done((bf16[1500,512]{1,0:T(8,128)(2,1)S(1)}, bf16[1500,512]{1,0:T(8,128)(2,1)}, u32[]{:S(2)}) %copy-start.2) | copy-done | bytes 1536024
  6.2 3.3 %whiten.1 = (f32[4224,128]{1,0:T(8,128)S(1)}, f32[3,512,128]{2,1,0:T(8,128)S(1)}, s32[19]{0:T(128)S(1)}) custom-call(s32[1]{0:T(128)} %bitcast.me_ref, s32[64]{0:T(128)S(1)} %copy-done.5, bf16[16,48,1500]{2,1,0:T(8,128)(2,1)S(1)} %copy-done, bf16[1500,512]{1,0:T(8,128)(2,1)S(1)} %copy-done.2, bf16[256,256]{1,0:T(8,128)(2,1)S(1)} %copy-done.4), custom_call_target="tpu_custom_call" | custom-call | flops 960233472 | bytes 8388608 | tf_op jit(solution)/shard_map/whiten/pallas_call | solution.py:326
  9.5 2.6 %finish.1 = (f32[4224,128]{1,0:T(8,128)S(1)}, f32[3,512,128]{2,1,0:T(8,128)S(1)}, bf16[32,16,384]{2,1,0:T(8,128)(2,1)}, bf16[32,16,384]{2,1,0:T(8,128)(2,1)}) custom-call(s32[19]{0:T(128)S(1)} %get-tuple-element.43.slot_ref, bf16[16,48,1500]{2,1,0:T(8,128)(2,1)S(1)} %copy-done.1, ...), custom_call_target="tpu_custom_call", output_to_operand_aliasing={{0}: (5, {}), {1}: (6, {})} | custom-call | tf_op jit(solution)/shard_map/finish/pallas_call | solution.py:340
  12.1 10.2 %all-to-all-start.1 = ((bf16[32,16,384]{2,1,0:T(8,128)(2,1)}), bf16[32,16,384]{2,1,0:T(8,128)(2,1)S(1)}, u32[]{:S(2)}, u32[]{:S(2)}) async-start(bf16[32,16,384]{2,1,0:T(8,128)(2,1)} %get-tuple-element.48), calls=%async_computation.1 | async-start | bytes 786432 | tf_op jit(solution)/shard_map/all_to_all | solution.py:353
  24.7 10.8 %all-to-all-done.1.rows_ref = bf16[32,16,384]{2,1,0:T(8,128)(2,1)S(1)} async-done(((bf16[32,16,384]{2,1,0:T(8,128)(2,1)}), bf16[32,16,384]{2,1,0:T(8,128)(2,1)S(1)}, u32[]{:S(2)}, u32[]{:S(2)}) %all-to-all-start.1) | async-done | bytes 393248 | tf_op jit(solution)/shard_map/all_to_all | solution.py:353
  36.3 1.6 %collective-permute-start.4 = (bf16[4,96,128]{2,1,0:T(8,128)(2,1)S(1)}, bf16[4,96,128]{2,1,0:T(8,128)(2,1)S(1)}, u32[]{:S(2)}, u32[]{:S(2)}) collective-permute-start(bf16[4,96,128]{2,1,0:T(8,128)(2,1)S(1)} %get-tuple-element.81.refs_0_), channel_id=1, source_target_pairs={{0,8},{1,9},{2,10},{3,11},{4,12},{5,13},{6,14},{7,15},{8,0},{9,1},... | collective-permute-start | bytes 294920 | tf_op jit(solution)/shard_map/ppermute | solution.py:252
  37.9 0.8 %collective-permute-start.3 = (bf16[4,96,128]{2,1,0:T(8,128)(2,1)S(1)}, bf16[4,96,128]{2,1,0:T(8,128)(2,1)S(1)}, u32[]{:S(2)}, u32[]{:S(2)}) collective-permute-start(bf16[4,96,128]{2,1,0:T(8,128)(2,1)S(1)} %get-tuple-element.81.refs_0_), channel_id=1, source_target_pairs={{0,2},{1,3},{2,0},{3,1},{4,6},{5,7},{6,4},{7,5},{8,10},{9,11},{10,... | collective-permute-start | bytes 294920 | tf_op jit(solution)/shard_map/ppermute | solution.py:252
  38.7 1.5 %collective-permute-start.2 = (bf16[4,96,128]{2,1,0:T(8,128)(2,1)S(1)}, bf16[4,96,128]{2,1,0:T(8,128)(2,1)S(1)}, u32[]{:S(2)}, u32[]{:S(2)}) collective-permute-start(bf16[4,96,128]{2,1,0:T(8,128)(2,1)S(1)} %get-tuple-element.81.refs_0_), channel_id=1, source_target_pairs={{0,4},{1,5},{2,6},{3,7},{4,0},{5,1},{6,2},{7,3},{8,12},{9,13},{10,... | collective-permute-start | bytes 294920 | tf_op jit(solution)/shard_map/ppermute | solution.py:252
  40.2 1.2 %collective-permute-start.1 = (bf16[4,96,128]{2,1,0:T(8,128)(2,1)S(1)}, bf16[4,96,128]{2,1,0:T(8,128)(2,1)S(1)}, u32[]{:S(2)}, u32[]{:S(2)}) collective-permute-start(bf16[4,96,128]{2,1,0:T(8,128)(2,1)S(1)} %get-tuple-element.81.refs_0_), channel_id=1, source_target_pairs={{0,6},{1,7},{2,4},{3,5},{4,2},{5,3},{6,0},{7,1},{8,14},{9,15},{10,... | collective-permute-start | bytes 294920 | tf_op jit(solution)/shard_map/ppermute | solution.py:252
  41.4 2.1 %collective-permute-done.5.refs_5_ = bf16[4,96,128]{2,1,0:T(8,128)(2,1)S(1)} collective-permute-done((bf16[4,96,128]{2,1,0:T(8,128)(2,1)S(1)}, bf16[4,96,128]{2,1,0:T(8,128)(2,1)S(1)}, u32[]{:S(2)}, u32[]{:S(2)}) %collective-permute-start.5) | collective-permute-done | bytes 98336 | tf_op jit(solution)/shard_map/ppermute | solution.py:252
  44.4 1.3 %collective-permute-done.1.refs_1_ = bf16[4,96,128]{2,1,0:T(8,128)(2,1)S(1)} collective-permute-done((bf16[4,96,128]{2,1,0:T(8,128)(2,1)S(1)}, bf16[4,96,128]{2,1,0:T(8,128)(2,1)S(1)}, u32[]{:S(2)}, u32[]{:S(2)}) %collective-permute-start.1) | collective-permute-done | bytes 98336 | tf_op jit(solution)/shard_map/ppermute | solution.py:252
  46.4 1.2 %collective-permute-start.7 = (bf16[8,96,128]{2,1,0:T(8,128)(2,1)S(1)}, bf16[8,96,128]{2,1,0:T(8,128)(2,1)S(1)}, u32[]{:S(2)}, u32[]{:S(2)}) collective-permute-start(bf16[8,96,128]{2,1,0:T(8,128)(2,1)S(1)} %get-tuple-element.78), channel_id=1, source_target_pairs={{0,4},{1,5},{2,6},{3,7},{4,0},{5,1},{6,2},{7,3},{8,12},{9,13},{10,... | collective-permute-start | bytes 589832 | tf_op jit(solution)/shard_map/ppermute | solution.py:252
  48.4 2.7 %collective-permute-start.8 = (bf16[4,96,128]{2,1,0:T(8,128)(2,1)S(1)}, bf16[4,96,128]{2,1,0:T(8,128)(2,1)S(1)}, u32[]{:S(2)}, u32[]{:S(2)}) collective-permute-start(bf16[4,96,128]{2,1,0:T(8,128)(2,1)S(1)} %collective-permute-done.1.refs_1_), channel_id=1, source_target_pairs={{0,16},{1,17},{2,18},{3,19},{4,20},{5,21},{6,22},{7,23},{8,24},{9,... | collective-permute-start | bytes 294920 | tf_op jit(solution)/shard_map/ppermute | solution.py:252
  51.1 2.0 %left.1.left_ref = bf16[128,64,128]{2,1,0:T(8,128)(2,1)S(1)} custom-call(f32[4224,128]{1,0:T(8,128)S(1)} %get-tuple-element.51.turned_ref), custom_call_target="tpu_custom_call" | custom-call | flops 10000000 | bytes 8388608 | tf_op jit(solution)/shard_map/left/pallas_call | solution.py:371
  53.4 1.6 %collective-permute-done.8.refs_3_ = bf16[4,96,128]{2,1,0:T(8,128)(2,1)S(1)} collective-permute-done((bf16[4,96,128]{2,1,0:T(8,128)(2,1)S(1)}, bf16[4,96,128]{2,1,0:T(8,128)(2,1)S(1)}, u32[]{:S(2)}, u32[]{:S(2)}) %collective-permute-start.8) | collective-permute-done | bytes 98336 | tf_op jit(solution)/shard_map/ppermute | solution.py:252
  55.2 1.4 %collective-permute-start.11 = (bf16[4,96,128]{2,1,0:T(8,128)(2,1)S(1)}, bf16[4,96,128]{2,1,0:T(8,128)(2,1)S(1)}, u32[]{:S(2)}, u32[]{:S(2)}) collective-permute-start(bf16[4,96,128]{2,1,0:T(8,128)(2,1)S(1)} %slice.8), channel_id=1, source_target_pairs={{0,4},{1,5},{2,6},{3,7},{4,0},{5,1},{6,2},{7,3},{8,12},{9,13},{10,... | collective-permute-start | bytes 294920 | tf_op jit(solution)/shard_map/ppermute | solution.py:252
  56.6 1.3 %collective-permute-start.12 = (bf16[4,96,128]{2,1,0:T(8,128)(2,1)S(1)}, bf16[4,96,128]{2,1,0:T(8,128)(2,1)S(1)}, u32[]{:S(2)}, u32[]{:S(2)}) collective-permute-start(bf16[4,96,128]{2,1,0:T(8,128)(2,1)S(1)} %collective-permute-done.8.refs_3_), channel_id=1, source_target_pairs={{0,8},{1,9},{2,10},{3,11},{4,12},{5,13},{6,14},{7,15},{8,0},{9,1},... | collective-permute-start | bytes 294920 | tf_op jit(solution)/shard_map/ppermute | solution.py:252
  58.3 2.2 %collective-permute-done.11.refs_3_ = bf16[4,96,128]{2,1,0:T(8,128)(2,1)S(1)} collective-permute-done((bf16[4,96,128]{2,1,0:T(8,128)(2,1)S(1)}, bf16[4,96,128]{2,1,0:T(8,128)(2,1)S(1)}, u32[]{:S(2)}, u32[]{:S(2)}) %collective-permute-start.11) | collective-permute-done | bytes 98336 | tf_op jit(solution)/shard_map/ppermute | solution.py:252
  60.5 1.0 %collective-permute-done.10.refs_2_ = bf16[4,96,128]{2,1,0:T(8,128)(2,1)S(1)} collective-permute-done((bf16[4,96,128]{2,1,0:T(8,128)(2,1)S(1)}, bf16[4,96,128]{2,1,0:T(8,128)(2,1)S(1)}, u32[]{:S(2)}, u32[]{:S(2)}) %collective-permute-start.10) | collective-permute-done | bytes 98336 | tf_op jit(solution)/shard_map/ppermute | solution.py:252
  62.2 1.0 %collective-permute-done.14.refs_0_ = bf16[12,96,128]{2,1,0:T(8,128)(2,1)S(1)} collective-permute-done((bf16[12,96,128]{2,1,0:T(8,128)(2,1)S(1)}, bf16[12,96,128]{2,1,0:T(8,128)(2,1)S(1)}, u32[]{:S(2)}, u32[]{:S(2)}) %collective-permute-start.14) | collective-permute-done | bytes 294944 | tf_op jit(solution)/shard_map/ppermute | solution.py:252
  63.2 1.9 %correlate.1 = (f32[2,64,16,256]{3,2,1,0:T(8,128)}, f32[4352,128]{1,0:T(8,128)S(1)}) custom-call(s32[1]{0:T(128)} %bitcast.me_ref, bf16[128,64,128]{2,1,0:T(8,128)(2,1)S(1)} %left.1.left_ref, f32[4352,128]{1,0:T(8,128)S(1)} %products.5._, bf16[12,96,128]{2,1,0:T(8,128)(2,1)S(1)} %collective-permute-done.14.refs_0_), custom_call_target="tpu_custom_call", output_to_operand_aliasing={{1}: (2, {})} | custom-call | tf_op jit(solution)/shard_map/correlate/pallas_call | solution.py:407
  (60 shorter events, 7.0 us)
Async XLA Ops:
  0.0 2.4 %copy-start.4 = (bf16[256,256]{1,0:T(8,128)(2,1)S(1)}, bf16[256,256]{1,0:T(8,128)(2,1)}, u32[]{:S(2)}) copy-start(bf16[256,256]{1,0:T(8,128)(2,1)} %constant.45.clone.band_ref) | copy-start | bytes 393220
  1.1 8.3 %collective-permute-start = (bf16[4,48,1500]{2,1,0:T(8,128)(2,1)S(1)}, bf16[4,48,1500]{2,1,0:T(8,128)(2,1)S(1)}, u32[]{:S(2)}, u32[]{:S(2)}) collective-permute-start(bf16[4,48,1500]{2,1,0:T(8,128)(2,1)S(1)} %slice.7), channel_id=1, source_target_pairs={{1,0},{2,1},{3,2},{4,3},{5,4},{6,5},{7,6},{8,7},{9,8},{10,9},{11,1... | collective-permute-start | bytes 1728008 | tf_op jit(solution)/shard_map/ppermute | solution.py:313
  2.5 1.7 %copy-start = (bf16[16,48,1500]{2,1,0:T(8,128)(2,1)S(1)}, bf16[16,48,1500]{2,1,0:T(8,128)(2,1)}, u32[]{:S(2)}) copy-start(bf16[16,48,1500]{2,1,0:T(8,128)(2,1)} %traces_ref.3) | copy-start | bytes 6912004
  4.1 1.4 %copy-start.2 = (bf16[1500,512]{1,0:T(8,128)(2,1)S(1)}, bf16[1500,512]{1,0:T(8,128)(2,1)}, u32[]{:S(2)}) copy-start(bf16[1500,512]{1,0:T(8,128)(2,1)} %constant.44.clone.table_ref) | copy-start | bytes 4608004
  5.5 0.7 %copy-start.5 = (s32[64]{0:T(128)S(1)}, s32[64]{0:T(128)}, u32[]{:S(2)}) copy-start(s32[64]{0:T(128)} %index_ref.1) | copy-start | bytes 772
  6.2 3.3 %copy-start.1 = (bf16[16,48,1500]{2,1,0:T(8,128)(2,1)S(1)}, bf16[16,48,1500]{2,1,0:T(8,128)(2,1)}, u32[]{:S(2)}) copy-start(bf16[16,48,1500]{2,1,0:T(8,128)(2,1)} %traces_ref.3) | copy-start | bytes 6912004
  6.2 3.3 %copy-start.3 = (bf16[1500,512]{1,0:T(8,128)(2,1)S(1)}, bf16[1500,512]{1,0:T(8,128)(2,1)}, u32[]{:S(2)}) copy-start(bf16[1500,512]{1,0:T(8,128)(2,1)} %constant.44.clone.table_ref) | copy-start | bytes 4608004
  9.5 12.9 %copy-start.6 = (s32[64]{0:T(128)S(1)}, s32[64]{0:T(128)}, u32[]{:S(2)}) copy-start(s32[64]{0:T(128)} %index_ref.1) | copy-start | bytes 772
  12.1 23.4 %all-to-all-start.1 = ((bf16[32,16,384]{2,1,0:T(8,128)(2,1)}), bf16[32,16,384]{2,1,0:T(8,128)(2,1)S(1)}, u32[]{:S(2)}, u32[]{:S(2)}) async-start(bf16[32,16,384]{2,1,0:T(8,128)(2,1)} %get-tuple-element.48), calls=%async_computation.1 | async-start | bytes 786432 | tf_op jit(solution)/shard_map/all_to_all | solution.py:353
  36.2 7.4 %collective-permute-start.5 = (bf16[4,96,128]{2,1,0:T(8,128)(2,1)S(1)}, bf16[4,96,128]{2,1,0:T(8,128)(2,1)S(1)}, u32[]{:S(2)}, u32[]{:S(2)}) collective-permute-start(bf16[4,96,128]{2,1,0:T(8,128)(2,1)S(1)} %get-tuple-element.81.refs_0_), channel_id=1, source_target_pairs={{0,16},{1,17},{2,18},{3,19},{4,20},{5,21},{6,22},{7,23},{8,24},{9,... | collective-permute-start | bytes 294920 | tf_op jit(solution)/shard_map/ppermute | solution.py:252
  36.3 7.3 %collective-permute-start.4 = (bf16[4,96,128]{2,1,0:T(8,128)(2,1)S(1)}, bf16[4,96,128]{2,1,0:T(8,128)(2,1)S(1)}, u32[]{:S(2)}, u32[]{:S(2)}) collective-permute-start(bf16[4,96,128]{2,1,0:T(8,128)(2,1)S(1)} %get-tuple-element.81.refs_0_), channel_id=1, source_target_pairs={{0,8},{1,9},{2,10},{3,11},{4,12},{5,13},{6,14},{7,15},{8,0},{9,1},... | collective-permute-start | bytes 294920 | tf_op jit(solution)/shard_map/ppermute | solution.py:252
  37.9 5.7 %collective-permute-start.3 = (bf16[4,96,128]{2,1,0:T(8,128)(2,1)S(1)}, bf16[4,96,128]{2,1,0:T(8,128)(2,1)S(1)}, u32[]{:S(2)}, u32[]{:S(2)}) collective-permute-start(bf16[4,96,128]{2,1,0:T(8,128)(2,1)S(1)} %get-tuple-element.81.refs_0_), channel_id=1, source_target_pairs={{0,2},{1,3},{2,0},{3,1},{4,6},{5,7},{6,4},{7,5},{8,10},{9,11},{10,... | collective-permute-start | bytes 294920 | tf_op jit(solution)/shard_map/ppermute | solution.py:252
  38.7 5.6 %collective-permute-start.2 = (bf16[4,96,128]{2,1,0:T(8,128)(2,1)S(1)}, bf16[4,96,128]{2,1,0:T(8,128)(2,1)S(1)}, u32[]{:S(2)}, u32[]{:S(2)}) collective-permute-start(bf16[4,96,128]{2,1,0:T(8,128)(2,1)S(1)} %get-tuple-element.81.refs_0_), channel_id=1, source_target_pairs={{0,4},{1,5},{2,6},{3,7},{4,0},{5,1},{6,2},{7,3},{8,12},{9,13},{10,... | collective-permute-start | bytes 294920 | tf_op jit(solution)/shard_map/ppermute | solution.py:252
  40.2 5.5 %collective-permute-start.1 = (bf16[4,96,128]{2,1,0:T(8,128)(2,1)S(1)}, bf16[4,96,128]{2,1,0:T(8,128)(2,1)S(1)}, u32[]{:S(2)}, u32[]{:S(2)}) collective-permute-start(bf16[4,96,128]{2,1,0:T(8,128)(2,1)S(1)} %get-tuple-element.81.refs_0_), channel_id=1, source_target_pairs={{0,6},{1,7},{2,4},{3,5},{4,2},{5,3},{6,0},{7,1},{8,14},{9,15},{10,... | collective-permute-start | bytes 294920 | tf_op jit(solution)/shard_map/ppermute | solution.py:252
  45.7 9.2 %collective-permute-start.9 = (bf16[8,96,128]{2,1,0:T(8,128)(2,1)S(1)}, bf16[8,96,128]{2,1,0:T(8,128)(2,1)S(1)}, u32[]{:S(2)}, u32[]{:S(2)}) collective-permute-start(bf16[8,96,128]{2,1,0:T(8,128)(2,1)S(1)} %pad_maximum_fusion.1), channel_id=1, source_target_pairs={{0,8},{1,9},{2,10},{3,11},{4,12},{5,13},{6,14},{7,15},{8,0},{9,1},... | collective-permute-start | bytes 589832 | tf_op jit(solution)/shard_map/ppermute | solution.py:252
  46.4 8.6 %collective-permute-start.7 = (bf16[8,96,128]{2,1,0:T(8,128)(2,1)S(1)}, bf16[8,96,128]{2,1,0:T(8,128)(2,1)S(1)}, u32[]{:S(2)}, u32[]{:S(2)}) collective-permute-start(bf16[8,96,128]{2,1,0:T(8,128)(2,1)S(1)} %get-tuple-element.78), channel_id=1, source_target_pairs={{0,4},{1,5},{2,6},{3,7},{4,0},{5,1},{6,2},{7,3},{8,12},{9,13},{10,... | collective-permute-start | bytes 589832 | tf_op jit(solution)/shard_map/ppermute | solution.py:252
  47.6 7.3 %collective-permute-start.6 = (bf16[8,96,128]{2,1,0:T(8,128)(2,1)S(1)}, bf16[8,96,128]{2,1,0:T(8,128)(2,1)S(1)}, u32[]{:S(2)}, u32[]{:S(2)}) collective-permute-start(bf16[8,96,128]{2,1,0:T(8,128)(2,1)S(1)} %get-tuple-element.78), channel_id=1, source_target_pairs={{0,2},{1,3},{2,0},{3,1},{4,6},{5,7},{6,4},{7,5},{8,10},{9,11},{10,... | collective-permute-start | bytes 589832 | tf_op jit(solution)/shard_map/ppermute | solution.py:252
  48.4 6.6 %collective-permute-start.8 = (bf16[4,96,128]{2,1,0:T(8,128)(2,1)S(1)}, bf16[4,96,128]{2,1,0:T(8,128)(2,1)S(1)}, u32[]{:S(2)}, u32[]{:S(2)}) collective-permute-start(bf16[4,96,128]{2,1,0:T(8,128)(2,1)S(1)} %collective-permute-done.1.refs_1_), channel_id=1, source_target_pairs={{0,16},{1,17},{2,18},{3,19},{4,20},{5,21},{6,22},{7,23},{8,24},{9,... | collective-permute-start | bytes 294920 | tf_op jit(solution)/shard_map/ppermute | solution.py:252
  55.1 6.5 %collective-permute-start.13 = (bf16[52,96,128]{2,1,0:T(8,128)(2,1)S(1)}, bf16[52,96,128]{2,1,0:T(8,128)(2,1)S(1)}, u32[]{:S(2)}, u32[]{:S(2)}) collective-permute-start(bf16[52,96,128]{2,1,0:T(8,128)(2,1)S(1)} %constant_dynamic-update-slice_fusion.2), channel_id=1, source_target_pairs={{0,1},{1,0},{2,3},{3,2},{4,5},{5,4},{6,7},{7,6},{8,9},{9,8},{10,11... | collective-permute-start | bytes 3833864 | tf_op jit(solution)/shard_map/ppermute | solution.py:252
  55.2 5.2 %collective-permute-start.11 = (bf16[4,96,128]{2,1,0:T(8,128)(2,1)S(1)}, bf16[4,96,128]{2,1,0:T(8,128)(2,1)S(1)}, u32[]{:S(2)}, u32[]{:S(2)}) collective-permute-start(bf16[4,96,128]{2,1,0:T(8,128)(2,1)S(1)} %slice.8), channel_id=1, source_target_pairs={{0,4},{1,5},{2,6},{3,7},{4,0},{5,1},{6,2},{7,3},{8,12},{9,13},{10,... | collective-permute-start | bytes 294920 | tf_op jit(solution)/shard_map/ppermute | solution.py:252
  56.6 4.9 %collective-permute-start.10 = (bf16[4,96,128]{2,1,0:T(8,128)(2,1)S(1)}, bf16[4,96,128]{2,1,0:T(8,128)(2,1)S(1)}, u32[]{:S(2)}, u32[]{:S(2)}) collective-permute-start(bf16[4,96,128]{2,1,0:T(8,128)(2,1)S(1)} %slice.8), channel_id=1, source_target_pairs={{0,2},{1,3},{2,0},{3,1},{4,6},{5,7},{6,4},{7,5},{8,10},{9,11},{10,... | collective-permute-start | bytes 294920 | tf_op jit(solution)/shard_map/ppermute | solution.py:252
  56.6 4.9 %collective-permute-start.12 = (bf16[4,96,128]{2,1,0:T(8,128)(2,1)S(1)}, bf16[4,96,128]{2,1,0:T(8,128)(2,1)S(1)}, u32[]{:S(2)}, u32[]{:S(2)}) collective-permute-start(bf16[4,96,128]{2,1,0:T(8,128)(2,1)S(1)} %collective-permute-done.8.refs_3_), channel_id=1, source_target_pairs={{0,8},{1,9},{2,10},{3,11},{4,12},{5,13},{6,14},{7,15},{8,0},{9,1},... | collective-permute-start | bytes 294920 | tf_op jit(solution)/shard_map/ppermute | solution.py:252
  61.6 1.6 %collective-permute-start.14 = (bf16[12,96,128]{2,1,0:T(8,128)(2,1)S(1)}, bf16[12,96,128]{2,1,0:T(8,128)(2,1)S(1)}, u32[]{:S(2)}, u32[]{:S(2)}) collective-permute-start(bf16[12,96,128]{2,1,0:T(8,128)(2,1)S(1)} %pad_maximum_fusion), channel_id=1, source_target_pairs={{0,1},{1,0},{2,3},{3,2},{4,5},{5,4},{6,7},{7,6},{8,9},{9,8},{10,11... | collective-permute-start | bytes 884744 | tf_op jit(solution)/shard_map/ppermute | solution.py:252
where the time goes:
time: 65.4 us; the launch traced here: 65.1 us
  starting transfers between devices  24.8 us (38%)
  waiting for transfers between devices  21 us (32%)
  Pallas kernels  11.5 us (18%)
  local copies, waits for them, and re-layouts  5.59 us (9%)
  other arithmetic  1.26 us (2%)
  between operations  0.93 us (1%)
    ppermute x14, starting transfers between devices, send(): lax.ppermute(pack(names), 'chan', route)  13.3 us
    all_to_all x1, waiting for transfers between devices, exchange(): rows = lax.all_to_all(rows, 'chan', 0, 0, tiled=True)  10.8 us
    all_to_all x1, starting transfers between devices, exchange(): rows = lax.all_to_all(rows, 'chan', 0, 0, tiled=True)  10.2 us
    ppermute x14, waiting for transfers between devices, send(): lax.ppermute(pack(names), 'chan', route)  10.2 us
    unnamed x23, local copies, waits for them, and re-layouts  3.93 us
    pallas_call x1, Pallas kernels, per_device(): pl.pallas_call(functools.partial(whiten_kernel, chans, slots), in_specs=[...  3.3 us
    pallas_call x1, Pallas kernels, per_device(): pl.pallas_call(functools.partial(finish_kernel, chans, slots), in_specs=[...  2.57 us
    pallas_call x1, Pallas kernels, per_device(): pl.pallas_call(functools.partial(left_kernel, chans, depth), in_specs=[vm...  1.97 us
  transfers between devices with their start and end apart: 16, of which 10 were waited for; matrix products, arithmetic and copies ran while one was open for 3% of the time, Pallas kernels for 10%

commit v1 on v0

--- a/solution.py
+++ b/solution.py
@@ -266,7 +266,7 @@
         multiply(*lists(near[:-1]))
         return lists(near[-1:])
 
-    first = [send(piece(0), flip) for flip in (x ^ y, y, x, z, zz)]
+    first = [send(piece(0), flip) for flip in (y, x, x ^ y, z, zz)]
     arrays = lax.optimization_barrier(lists(first)[0])
     near += [keep(array, names) for array, (_, names) in zip(arrays, first)]
     mid = [

time: 65.4 us -> 66.4 us (1.015)
  waiting for transfers between devices: 21 us -> 21.7 us
  transfers between devices with their start and end apart: 16 -> 16, of which waited for: 10 -> 11; matrix products, arithmetic and copies ran while one was open for 3% -> 3% of each run, Pallas kernels for 10% -> 10%
where the time goes in v1:
time: 66.4 us; the launch traced here: 66.1 us
  starting transfers between devices  25 us (38%)
  waiting for transfers between devices  21.7 us (33%)
  Pallas kernels  11.6 us (17%)
  local copies, waits for them, and re-layouts  5.59 us (8%)
  other arithmetic  1.26 us (2%)
  between operations  0.93 us (1%)
    ppermute x14, starting transfers between devices, send(): lax.ppermute(pack(names), 'chan', route)  13.5 us
    ppermute x14, waiting for transfers between devices, send(): lax.ppermute(pack(names), 'chan', route)  10.9 us
    all_to_all x1, waiting for transfers between devices, exchange(): rows = lax.all_to_all(rows, 'chan', 0, 0, tiled=True)  10.8 us
    all_to_all x1, starting transfers between devices, exchange(): rows = lax.all_to_all(rows, 'chan', 0, 0, tiled=True)  10.2 us
    unnamed x23, local copies, waits for them, and re-layouts  3.93 us
    pallas_call x1, Pallas kernels, per_device(): pl.pallas_call(functools.partial(whiten_kernel, chans, slots), in_specs=[...  3.53 us
    pallas_call x1, Pallas kernels, per_device(): pl.pallas_call(functools.partial(finish_kernel, chans, slots), in_specs=[...  2.46 us
    pallas_call x1, Pallas kernels, per_device(): pl.pallas_call(functools.partial(left_kernel, chans, depth), in_specs=[vm...  1.97 us
  transfers between devices with their start and end apart: 16, of which 11 were waited for; matrix products, arithmetic and copies ran while one was open for 3% of the time, Pallas kernels for 10%

profile of v1, /device:TPU:0, one launch (start us, length us, event | category | flops | bytes accessed | tf_op | source)
XLA Modules:
  0.0 66.1 jit_solution(496006487267566784)
XLA Ops:
  0.0 1.1 %slice.7 = bf16[4,48,1500]{2,1,0:T(8,128)(2,1)S(1)} slice(bf16[16,48,1500]{2,1,0:T(8,128)(2,1)} %traces_ref.3), slice={[0:4], [0:48], [0:1500]} | slice | bytes 1152000 | tf_op jit(solution)/shard_map/slice | solution.py:313
  1.1 1.3 %collective-permute-start = (bf16[4,48,1500]{2,1,0:T(8,128)(2,1)S(1)}, bf16[4,48,1500]{2,1,0:T(8,128)(2,1)S(1)}, u32[]{:S(2)}, u32[]{:S(2)}) collective-permute-start(bf16[4,48,1500]{2,1,0:T(8,128)(2,1)S(1)} %slice.7), channel_id=1, source_target_pairs={{1,0},{2,1},{3,2},{4,3},{5,4},{6,5},{7,6},{8,7},{9,8},{10,9},{11,1... | collective-permute-start | bytes 1728008 | tf_op jit(solution)/shard_map/ppermute | solution.py:313
  2.5 1.7 %copy-done = bf16[16,48,1500]{2,1,0:T(8,128)(2,1)S(1)} copy-done((bf16[16,48,1500]{2,1,0:T(8,128)(2,1)S(1)}, bf16[16,48,1500]{2,1,0:T(8,128)(2,1)}, u32[]{:S(2)}) %copy-start) | copy-done | bytes 2304024
  4.1 1.4 %copy-done.2 = bf16[1500,512]{1,0:T(8,128)(2,1)S(1)} copy-done((bf16[1500,512]{1,0:T(8,128)(2,1)S(1)}, bf16[1500,512]{1,0:T(8,128)(2,1)}, u32[]{:S(2)}) %copy-start.2) | copy-done | bytes 1536024
  6.2 3.5 %whiten.1 = (f32[4224,128]{1,0:T(8,128)S(1)}, f32[3,512,128]{2,1,0:T(8,128)S(1)}, s32[19]{0:T(128)S(1)}) custom-call(s32[1]{0:T(128)} %bitcast.me_ref, s32[64]{0:T(128)S(1)} %copy-done.5, bf16[16,48,1500]{2,1,0:T(8,128)(2,1)S(1)} %copy-done, bf16[1500,512]{1,0:T(8,128)(2,1)S(1)} %copy-done.2, bf16[256,256]{1,0:T(8,128)(2,1)S(1)} %copy-done.4), custom_call_target="tpu_custom_call" | custom-call | flops 960233472 | bytes 8388608 | tf_op jit(solution)/shard_map/whiten/pallas_call | solution.py:326
  9.8 2.5 %finish.1 = (f32[4224,128]{1,0:T(8,128)S(1)}, f32[3,512,128]{2,1,0:T(8,128)S(1)}, bf16[32,16,384]{2,1,0:T(8,128)(2,1)}, bf16[32,16,384]{2,1,0:T(8,128)(2,1)}) custom-call(s32[19]{0:T(128)S(1)} %get-tuple-element.43.slot_ref, bf16[16,48,1500]{2,1,0:T(8,128)(2,1)S(1)} %copy-done.1, ...), custom_call_target="tpu_custom_call", output_to_operand_aliasing={{0}: (5, {}), {1}: (6, {})} | custom-call | tf_op jit(solution)/shard_map/finish/pallas_call | solution.py:340
  12.2 10.2 %all-to-all-start.1 = ((bf16[32,16,384]{2,1,0:T(8,128)(2,1)}), bf16[32,16,384]{2,1,0:T(8,128)(2,1)S(1)}, u32[]{:S(2)}, u32[]{:S(2)}) async-start(bf16[32,16,384]{2,1,0:T(8,128)(2,1)} %get-tuple-element.48), calls=%async_computation.1 | async-start | bytes 786432 | tf_op jit(solution)/shard_map/all_to_all | solution.py:353
  24.8 10.8 %all-to-all-done.1.rows_ref = bf16[32,16,384]{2,1,0:T(8,128)(2,1)S(1)} async-done(((bf16[32,16,384]{2,1,0:T(8,128)(2,1)}), bf16[32,16,384]{2,1,0:T(8,128)(2,1)S(1)}, u32[]{:S(2)}, u32[]{:S(2)}) %all-to-all-start.1) | async-done | bytes 393248 | tf_op jit(solution)/shard_map/all_to_all | solution.py:353
  36.4 1.6 %collective-permute-start.4 = (bf16[4,96,128]{2,1,0:T(8,128)(2,1)S(1)}, bf16[4,96,128]{2,1,0:T(8,128)(2,1)S(1)}, u32[]{:S(2)}, u32[]{:S(2)}) collective-permute-start(bf16[4,96,128]{2,1,0:T(8,128)(2,1)S(1)} %get-tuple-element.81.refs_0_), channel_id=1, source_target_pairs={{0,8},{1,9},{2,10},{3,11},{4,12},{5,13},{6,14},{7,15},{8,0},{9,1},... | collective-permute-start | bytes 294920 | tf_op jit(solution)/shard_map/ppermute | solution.py:252
  38.0 1.7 %collective-permute-start.3 = (bf16[4,96,128]{2,1,0:T(8,128)(2,1)S(1)}, bf16[4,96,128]{2,1,0:T(8,128)(2,1)S(1)}, u32[]{:S(2)}, u32[]{:S(2)}) collective-permute-start(bf16[4,96,128]{2,1,0:T(8,128)(2,1)S(1)} %get-tuple-element.81.refs_0_), channel_id=1, source_target_pairs={{0,6},{1,7},{2,4},{3,5},{4,2},{5,3},{6,0},{7,1},{8,14},{9,15},{10,... | collective-permute-start | bytes 294920 | tf_op jit(solution)/shard_map/ppermute | solution.py:252
  40.4 1.1 %collective-permute-start.1 = (bf16[4,96,128]{2,1,0:T(8,128)(2,1)S(1)}, bf16[4,96,128]{2,1,0:T(8,128)(2,1)S(1)}, u32[]{:S(2)}, u32[]{:S(2)}) collective-permute-start(bf16[4,96,128]{2,1,0:T(8,128)(2,1)S(1)} %get-tuple-element.81.refs_0_), channel_id=1, source_target_pairs={{0,4},{1,5},{2,6},{3,7},{4,0},{5,1},{6,2},{7,3},{8,12},{9,13},{10,... | collective-permute-start | bytes 294920 | tf_op jit(solution)/shard_map/ppermute | solution.py:252
  41.5 2.1 %collective-permute-done.5.refs_5_ = bf16[4,96,128]{2,1,0:T(8,128)(2,1)S(1)} collective-permute-done((bf16[4,96,128]{2,1,0:T(8,128)(2,1)S(1)}, bf16[4,96,128]{2,1,0:T(8,128)(2,1)S(1)}, u32[]{:S(2)}, u32[]{:S(2)}) %collective-permute-start.5) | collective-permute-done | bytes 98336 | tf_op jit(solution)/shard_map/ppermute | solution.py:252
  45.2 1.5 %collective-permute-start.9 = (bf16[8,96,128]{2,1,0:T(8,128)(2,1)S(1)}, bf16[8,96,128]{2,1,0:T(8,128)(2,1)S(1)}, u32[]{:S(2)}, u32[]{:S(2)}) collective-permute-start(bf16[8,96,128]{2,1,0:T(8,128)(2,1)S(1)} %pad_maximum_fusion.1), channel_id=1, source_target_pairs={{0,8},{1,9},{2,10},{3,11},{4,12},{5,13},{6,14},{7,15},{8,0},{9,1},... | collective-permute-start | bytes 589832 | tf_op jit(solution)/shard_map/ppermute | solution.py:252
  46.8 0.8 %collective-permute-start.7 = (bf16[8,96,128]{2,1,0:T(8,128)(2,1)S(1)}, bf16[8,96,128]{2,1,0:T(8,128)(2,1)S(1)}, u32[]{:S(2)}, u32[]{:S(2)}) collective-permute-start(bf16[8,96,128]{2,1,0:T(8,128)(2,1)S(1)} %get-tuple-element.78), channel_id=1, source_target_pairs={{0,4},{1,5},{2,6},{3,7},{4,0},{5,1},{6,2},{7,3},{8,12},{9,13},{10,... | collective-permute-start | bytes 589832 | tf_op jit(solution)/shard_map/ppermute | solution.py:252
  48.3 2.4 %collective-permute-start.8 = (bf16[4,96,128]{2,1,0:T(8,128)(2,1)S(1)}, bf16[4,96,128]{2,1,0:T(8,128)(2,1)S(1)}, u32[]{:S(2)}, u32[]{:S(2)}) collective-permute-start(bf16[4,96,128]{2,1,0:T(8,128)(2,1)S(1)} %collective-permute-done.3.refs_3_), channel_id=1, source_target_pairs={{0,16},{1,17},{2,18},{3,19},{4,20},{5,21},{6,22},{7,23},{8,24},{9,... | collective-permute-start | bytes 294920 | tf_op jit(solution)/shard_map/ppermute | solution.py:252
  50.7 2.0 %left.1.left_ref = bf16[128,64,128]{2,1,0:T(8,128)(2,1)S(1)} custom-call(f32[4224,128]{1,0:T(8,128)S(1)} %get-tuple-element.51.turned_ref), custom_call_target="tpu_custom_call" | custom-call | flops 10000000 | bytes 8388608 | tf_op jit(solution)/shard_map/left/pallas_call | solution.py:371
  53.0 1.9 %collective-permute-done.8.refs_3_ = bf16[4,96,128]{2,1,0:T(8,128)(2,1)S(1)} collective-permute-done((bf16[4,96,128]{2,1,0:T(8,128)(2,1)S(1)}, bf16[4,96,128]{2,1,0:T(8,128)(2,1)S(1)}, u32[]{:S(2)}, u32[]{:S(2)}) %collective-permute-start.8) | collective-permute-done | bytes 98336 | tf_op jit(solution)/shard_map/ppermute | solution.py:252
  55.1 1.1 %collective-permute-start.11 = (bf16[4,96,128]{2,1,0:T(8,128)(2,1)S(1)}, bf16[4,96,128]{2,1,0:T(8,128)(2,1)S(1)}, u32[]{:S(2)}, u32[]{:S(2)}) collective-permute-start(bf16[4,96,128]{2,1,0:T(8,128)(2,1)S(1)} %slice.8), channel_id=1, source_target_pairs={{0,4},{1,5},{2,6},{3,7},{4,0},{5,1},{6,2},{7,3},{8,12},{9,13},{10,... | collective-permute-start | bytes 294920 | tf_op jit(solution)/shard_map/ppermute | solution.py:252
  56.3 1.6 %collective-permute-start.10 = (bf16[4,96,128]{2,1,0:T(8,128)(2,1)S(1)}, bf16[4,96,128]{2,1,0:T(8,128)(2,1)S(1)}, u32[]{:S(2)}, u32[]{:S(2)}) collective-permute-start(bf16[4,96,128]{2,1,0:T(8,128)(2,1)S(1)} %slice.8), channel_id=1, source_target_pairs={{0,2},{1,3},{2,0},{3,1},{4,6},{5,7},{6,4},{7,5},{8,10},{9,11},{10,... | collective-permute-start | bytes 294920 | tf_op jit(solution)/shard_map/ppermute | solution.py:252
  58.2 2.2 %collective-permute-done.11.refs_3_ = bf16[4,96,128]{2,1,0:T(8,128)(2,1)S(1)} collective-permute-done((bf16[4,96,128]{2,1,0:T(8,128)(2,1)S(1)}, bf16[4,96,128]{2,1,0:T(8,128)(2,1)S(1)}, u32[]{:S(2)}, u32[]{:S(2)}) %collective-permute-start.11) | collective-permute-done | bytes 98336 | tf_op jit(solution)/shard_map/ppermute | solution.py:252
  60.4 0.8 %collective-permute-done.10.refs_2_ = bf16[4,96,128]{2,1,0:T(8,128)(2,1)S(1)} collective-permute-done((bf16[4,96,128]{2,1,0:T(8,128)(2,1)S(1)}, bf16[4,96,128]{2,1,0:T(8,128)(2,1)S(1)}, u32[]{:S(2)}, u32[]{:S(2)}) %collective-permute-start.10) | collective-permute-done | bytes 98336 | tf_op jit(solution)/shard_map/ppermute | solution.py:252
  61.2 1.4 %collective-permute-done.12.refs_4_ = bf16[4,96,128]{2,1,0:T(8,128)(2,1)S(1)} collective-permute-done((bf16[4,96,128]{2,1,0:T(8,128)(2,1)S(1)}, bf16[4,96,128]{2,1,0:T(8,128)(2,1)S(1)}, u32[]{:S(2)}, u32[]{:S(2)}) %collective-permute-start.12) | collective-permute-done | bytes 98336 | tf_op jit(solution)/shard_map/ppermute | solution.py:252
  63.2 1.0 %collective-permute-done.14.refs_0_ = bf16[12,96,128]{2,1,0:T(8,128)(2,1)S(1)} collective-permute-done((bf16[12,96,128]{2,1,0:T(8,128)(2,1)S(1)}, bf16[12,96,128]{2,1,0:T(8,128)(2,1)S(1)}, u32[]{:S(2)}, u32[]{:S(2)}) %collective-permute-start.14) | collective-permute-done | bytes 294944 | tf_op jit(solution)/shard_map/ppermute | solution.py:252
  64.2 1.9 %correlate.1 = (f32[2,64,16,256]{3,2,1,0:T(8,128)}, f32[4352,128]{1,0:T(8,128)S(1)}) custom-call(s32[1]{0:T(128)} %bitcast.me_ref, bf16[128,64,128]{2,1,0:T(8,128)(2,1)S(1)} %left.1.left_ref, f32[4352,128]{1,0:T(8,128)S(1)} %products.5._, bf16[12,96,128]{2,1,0:T(8,128)(2,1)S(1)} %collective-permute-done.14.refs_0_), custom_call_target="tpu_custom_call", output_to_operand_aliasing={{1}: (2, {})} | custom-call | tf_op jit(solution)/shard_map/correlate/pallas_call | solution.py:407
  (60 shorter events, 7.6 us)
Async XLA Ops:
  0.0 2.4 %copy-start.4 = (bf16[256,256]{1,0:T(8,128)(2,1)S(1)}, bf16[256,256]{1,0:T(8,128)(2,1)}, u32[]{:S(2)}) copy-start(bf16[256,256]{1,0:T(8,128)(2,1)} %constant.45.clone.band_ref) | copy-start | bytes 393220
  1.1 8.6 %collective-permute-start = (bf16[4,48,1500]{2,1,0:T(8,128)(2,1)S(1)}, bf16[4,48,1500]{2,1,0:T(8,128)(2,1)S(1)}, u32[]{:S(2)}, u32[]{:S(2)}) collective-permute-start(bf16[4,48,1500]{2,1,0:T(8,128)(2,1)S(1)} %slice.7), channel_id=1, source_target_pairs={{1,0},{2,1},{3,2},{4,3},{5,4},{6,5},{7,6},{8,7},{9,8},{10,9},{11,1... | collective-permute-start | bytes 1728008 | tf_op jit(solution)/shard_map/ppermute | solution.py:313
  2.5 1.7 %copy-start = (bf16[16,48,1500]{2,1,0:T(8,128)(2,1)S(1)}, bf16[16,48,1500]{2,1,0:T(8,128)(2,1)}, u32[]{:S(2)}) copy-start(bf16[16,48,1500]{2,1,0:T(8,128)(2,1)} %traces_ref.3) | copy-start | bytes 6912004
  4.1 1.4 %copy-start.2 = (bf16[1500,512]{1,0:T(8,128)(2,1)S(1)}, bf16[1500,512]{1,0:T(8,128)(2,1)}, u32[]{:S(2)}) copy-start(bf16[1500,512]{1,0:T(8,128)(2,1)} %constant.44.clone.table_ref) | copy-start | bytes 4608004
  5.5 0.7 copy-start.5
  6.2 3.6 %copy-start.1 = (bf16[16,48,1500]{2,1,0:T(8,128)(2,1)S(1)}, bf16[16,48,1500]{2,1,0:T(8,128)(2,1)}, u32[]{:S(2)}) copy-start(bf16[16,48,1500]{2,1,0:T(8,128)(2,1)} %traces_ref.3) | copy-start | bytes 6912004
  6.2 3.6 %copy-start.3 = (bf16[1500,512]{1,0:T(8,128)(2,1)S(1)}, bf16[1500,512]{1,0:T(8,128)(2,1)}, u32[]{:S(2)}) copy-start(bf16[1500,512]{1,0:T(8,128)(2,1)} %constant.44.clone.table_ref) | copy-start | bytes 4608004
  9.8 12.8 %copy-start.6 = (s32[64]{0:T(128)S(1)}, s32[64]{0:T(128)}, u32[]{:S(2)}) copy-start(s32[64]{0:T(128)} %index_ref.1) | copy-start | bytes 772
  12.2 23.4 %all-to-all-start.1 = ((bf16[32,16,384]{2,1,0:T(8,128)(2,1)}), bf16[32,16,384]{2,1,0:T(8,128)(2,1)S(1)}, u32[]{:S(2)}, u32[]{:S(2)}) async-start(bf16[32,16,384]{2,1,0:T(8,128)(2,1)} %get-tuple-element.48), calls=%async_computation.1 | async-start | bytes 786432 | tf_op jit(solution)/shard_map/all_to_all | solution.py:353
  36.3 7.4 %collective-permute-start.5 = (bf16[4,96,128]{2,1,0:T(8,128)(2,1)S(1)}, bf16[4,96,128]{2,1,0:T(8,128)(2,1)S(1)}, u32[]{:S(2)}, u32[]{:S(2)}) collective-permute-start(bf16[4,96,128]{2,1,0:T(8,128)(2,1)S(1)} %get-tuple-element.81.refs_0_), channel_id=1, source_target_pairs={{0,16},{1,17},{2,18},{3,19},{4,20},{5,21},{6,22},{7,23},{8,24},{9,... | collective-permute-start | bytes 294920 | tf_op jit(solution)/shard_map/ppermute | solution.py:252
  36.4 7.3 %collective-permute-start.4 = (bf16[4,96,128]{2,1,0:T(8,128)(2,1)S(1)}, bf16[4,96,128]{2,1,0:T(8,128)(2,1)S(1)}, u32[]{:S(2)}, u32[]{:S(2)}) collective-permute-start(bf16[4,96,128]{2,1,0:T(8,128)(2,1)S(1)} %get-tuple-element.81.refs_0_), channel_id=1, source_target_pairs={{0,8},{1,9},{2,10},{3,11},{4,12},{5,13},{6,14},{7,15},{8,0},{9,1},... | collective-permute-start | bytes 294920 | tf_op jit(solution)/shard_map/ppermute | solution.py:252
  38.0 6.1 %collective-permute-start.3 = (bf16[4,96,128]{2,1,0:T(8,128)(2,1)S(1)}, bf16[4,96,128]{2,1,0:T(8,128)(2,1)S(1)}, u32[]{:S(2)}, u32[]{:S(2)}) collective-permute-start(bf16[4,96,128]{2,1,0:T(8,128)(2,1)S(1)} %get-tuple-element.81.refs_0_), channel_id=1, source_target_pairs={{0,6},{1,7},{2,4},{3,5},{4,2},{5,3},{6,0},{7,1},{8,14},{9,15},{10,... | collective-permute-start | bytes 294920 | tf_op jit(solution)/shard_map/ppermute | solution.py:252
  39.8 4.8 %collective-permute-start.2 = (bf16[4,96,128]{2,1,0:T(8,128)(2,1)S(1)}, bf16[4,96,128]{2,1,0:T(8,128)(2,1)S(1)}, u32[]{:S(2)}, u32[]{:S(2)}) collective-permute-start(bf16[4,96,128]{2,1,0:T(8,128)(2,1)S(1)} %get-tuple-element.81.refs_0_), channel_id=1, source_target_pairs={{0,2},{1,3},{2,0},{3,1},{4,6},{5,7},{6,4},{7,5},{8,10},{9,11},{10,... | collective-permute-start | bytes 294920 | tf_op jit(solution)/shard_map/ppermute | solution.py:252
  40.4 4.7 %collective-permute-start.1 = (bf16[4,96,128]{2,1,0:T(8,128)(2,1)S(1)}, bf16[4,96,128]{2,1,0:T(8,128)(2,1)S(1)}, u32[]{:S(2)}, u32[]{:S(2)}) collective-permute-start(bf16[4,96,128]{2,1,0:T(8,128)(2,1)S(1)} %get-tuple-element.81.refs_0_), channel_id=1, source_target_pairs={{0,4},{1,5},{2,6},{3,7},{4,0},{5,1},{6,2},{7,3},{8,12},{9,13},{10,... | collective-permute-start | bytes 294920 | tf_op jit(solution)/shard_map/ppermute | solution.py:252
  45.2 9.7 %collective-permute-start.9 = (bf16[8,96,128]{2,1,0:T(8,128)(2,1)S(1)}, bf16[8,96,128]{2,1,0:T(8,128)(2,1)S(1)}, u32[]{:S(2)}, u32[]{:S(2)}) collective-permute-start(bf16[8,96,128]{2,1,0:T(8,128)(2,1)S(1)} %pad_maximum_fusion.1), channel_id=1, source_target_pairs={{0,8},{1,9},{2,10},{3,11},{4,12},{5,13},{6,14},{7,15},{8,0},{9,1},... | collective-permute-start | bytes 589832 | tf_op jit(solution)/shard_map/ppermute | solution.py:252
  46.8 8.1 %collective-permute-start.7 = (bf16[8,96,128]{2,1,0:T(8,128)(2,1)S(1)}, bf16[8,96,128]{2,1,0:T(8,128)(2,1)S(1)}, u32[]{:S(2)}, u32[]{:S(2)}) collective-permute-start(bf16[8,96,128]{2,1,0:T(8,128)(2,1)S(1)} %get-tuple-element.78), channel_id=1, source_target_pairs={{0,4},{1,5},{2,6},{3,7},{4,0},{5,1},{6,2},{7,3},{8,12},{9,13},{10,... | collective-permute-start | bytes 589832 | tf_op jit(solution)/shard_map/ppermute | solution.py:252
  47.7 7.2 %collective-permute-start.6 = (bf16[8,96,128]{2,1,0:T(8,128)(2,1)S(1)}, bf16[8,96,128]{2,1,0:T(8,128)(2,1)S(1)}, u32[]{:S(2)}, u32[]{:S(2)}) collective-permute-start(bf16[8,96,128]{2,1,0:T(8,128)(2,1)S(1)} %get-tuple-element.78), channel_id=1, source_target_pairs={{0,2},{1,3},{2,0},{3,1},{4,6},{5,7},{6,4},{7,5},{8,10},{9,11},{10,... | collective-permute-start | bytes 589832 | tf_op jit(solution)/shard_map/ppermute | solution.py:252
  48.3 6.6 %collective-permute-start.8 = (bf16[4,96,128]{2,1,0:T(8,128)(2,1)S(1)}, bf16[4,96,128]{2,1,0:T(8,128)(2,1)S(1)}, u32[]{:S(2)}, u32[]{:S(2)}) collective-permute-start(bf16[4,96,128]{2,1,0:T(8,128)(2,1)S(1)} %collective-permute-done.3.refs_3_), channel_id=1, source_target_pairs={{0,16},{1,17},{2,18},{3,19},{4,20},{5,21},{6,22},{7,23},{8,24},{9,... | collective-permute-start | bytes 294920 | tf_op jit(solution)/shard_map/ppermute | solution.py:252
  55.0 7.6 %collective-permute-start.13 = (bf16[52,96,128]{2,1,0:T(8,128)(2,1)S(1)}, bf16[52,96,128]{2,1,0:T(8,128)(2,1)S(1)}, u32[]{:S(2)}, u32[]{:S(2)}) collective-permute-start(bf16[52,96,128]{2,1,0:T(8,128)(2,1)S(1)} %constant_dynamic-update-slice_fusion.2), channel_id=1, source_target_pairs={{0,1},{1,0},{2,3},{3,2},{4,5},{5,4},{6,7},{7,6},{8,9},{9,8},{10,11... | collective-permute-start | bytes 3833864 | tf_op jit(solution)/shard_map/ppermute | solution.py:252
  55.1 5.2 %collective-permute-start.11 = (bf16[4,96,128]{2,1,0:T(8,128)(2,1)S(1)}, bf16[4,96,128]{2,1,0:T(8,128)(2,1)S(1)}, u32[]{:S(2)}, u32[]{:S(2)}) collective-permute-start(bf16[4,96,128]{2,1,0:T(8,128)(2,1)S(1)} %slice.8), channel_id=1, source_target_pairs={{0,4},{1,5},{2,6},{3,7},{4,0},{5,1},{6,2},{7,3},{8,12},{9,13},{10,... | collective-permute-start | bytes 294920 | tf_op jit(solution)/shard_map/ppermute | solution.py:252
  56.3 4.9 %collective-permute-start.10 = (bf16[4,96,128]{2,1,0:T(8,128)(2,1)S(1)}, bf16[4,96,128]{2,1,0:T(8,128)(2,1)S(1)}, u32[]{:S(2)}, u32[]{:S(2)}) collective-permute-start(bf16[4,96,128]{2,1,0:T(8,128)(2,1)S(1)} %slice.8), channel_id=1, source_target_pairs={{0,2},{1,3},{2,0},{3,1},{4,6},{5,7},{6,4},{7,5},{8,10},{9,11},{10,... | collective-permute-start | bytes 294920 | tf_op jit(solution)/shard_map/ppermute | solution.py:252
  57.9 4.6 %collective-permute-start.12 = (bf16[4,96,128]{2,1,0:T(8,128)(2,1)S(1)}, bf16[4,96,128]{2,1,0:T(8,128)(2,1)S(1)}, u32[]{:S(2)}, u32[]{:S(2)}) collective-permute-start(bf16[4,96,128]{2,1,0:T(8,128)(2,1)S(1)} %collective-permute-done.8.refs_3_), channel_id=1, source_target_pairs={{0,8},{1,9},{2,10},{3,11},{4,12},{5,13},{6,14},{7,15},{8,0},{9,1},... | collective-permute-start | bytes 294920 | tf_op jit(solution)/shard_map/ppermute | solution.py:252
  62.6 1.6 %collective-permute-start.14 = (bf16[12,96,128]{2,1,0:T(8,128)(2,1)S(1)}, bf16[12,96,128]{2,1,0:T(8,128)(2,1)S(1)}, u32[]{:S(2)}, u32[]{:S(2)}) collective-permute-start(bf16[12,96,128]{2,1,0:T(8,128)(2,1)S(1)} %pad_maximum_fusion), channel_id=1, source_target_pairs={{0,1},{1,0},{2,3},{3,2},{4,5},{5,4},{6,7},{7,6},{8,9},{9,8},{10,11... | collective-permute-start | bytes 884744 | tf_op jit(solution)/shard_map/ppermute | solution.py:252

commit v2 on v0

--- a/solution.py
+++ b/solution.py
@@ -285,12 +285,13 @@
     ]
     theirs = send([name for pair in near + mid for name in pair[1]], core)
     multiply(*lists(mid))
-    arrays = after_products(*lists(last)[0])
+    arrays = lists(last)[0]
+    arrays[-1:] = after_products(arrays[-1])
     last = [keep(array, names) for array, (_, names) in zip(arrays, last)]
     assert sorted(place) == [(f, g) for f in range(0, n, 2) for g in range(groups)]
-    final = send([name for pair in last for name in pair[1]], core)
+    final = [send(names, core) for _, names in last]
     multiply(*lists([theirs] + last))
-    return lists([final])
+    return lists(final)
 
 
 def plan_places(source_index, chans, slots):

time: 65.4 us -> 65.2 us (level)
  waiting for transfers between devices: 21 us -> 20.3 us
    ppermute x14 -> x16, waiting for transfers between devices: 10.2 us -> 9.51 us  [send(): lax.ppermute(pack(names), 'chan', route)]
    ppermute x14 -> x16, starting transfers between devices: 13.3 us -> 13.8 us  [send(): lax.ppermute(pack(names), 'chan', route)]
  transfers between devices with their start and end apart: 16 -> 18, of which waited for: 10 -> 11; matrix products, arithmetic and copies ran while one was open for 3% -> 3% of each run, Pallas kernels for 10% -> 10%
where the time goes in v2:
time: 65.2 us; the launch traced here: 64.9 us
  starting transfers between devices  25.4 us (39%)
  waiting for transfers between devices  20.3 us (31%)
  Pallas kernels  11.4 us (17%)
  local copies, waits for them, and re-layouts  5.59 us (9%)
  other arithmetic  1.25 us (2%)
  between operations  0.96 us (1%)
    ppermute x16, starting transfers between devices, send(): lax.ppermute(pack(names), 'chan', route)  13.8 us
    all_to_all x1, waiting for transfers between devices, exchange(): rows = lax.all_to_all(rows, 'chan', 0, 0, tiled=True)  10.7 us
    all_to_all x1, starting transfers between devices, exchange(): rows = lax.all_to_all(rows, 'chan', 0, 0, tiled=True)  10.3 us
    ppermute x16, waiting for transfers between devices, send(): lax.ppermute(pack(names), 'chan', route)  9.51 us
    unnamed x23, local copies, waits for them, and re-layouts  3.93 us
    pallas_call x1, Pallas kernels, per_device(): pl.pallas_call(functools.partial(whiten_kernel, chans, slots), in_specs=[...  3.3 us
    pallas_call x1, Pallas kernels, per_device(): pl.pallas_call(functools.partial(finish_kernel, chans, slots), in_specs=[...  2.46 us
    pallas_call x1, Pallas kernels, per_device(): pl.pallas_call(functools.partial(left_kernel, chans, depth), in_specs=[vm...  1.97 us
  transfers between devices with their start and end apart: 18, of which 11 were waited for; matrix products, arithmetic and copies ran while one was open for 3% of the time, Pallas kernels for 10%

profile of v2, /device:TPU:0, one launch (start us, length us, event | category | flops | bytes accessed | tf_op | source)
XLA Modules:
  0.0 64.9 jit_solution(592468902456721814)
XLA Ops:
  0.0 1.1 %slice.7 = bf16[4,48,1500]{2,1,0:T(8,128)(2,1)S(1)} slice(bf16[16,48,1500]{2,1,0:T(8,128)(2,1)} %traces_ref.3), slice={[0:4], [0:48], [0:1500]} | slice | bytes 1152000 | tf_op jit(solution)/shard_map/slice | solution.py:314
  1.1 1.3 %collective-permute-start = (bf16[4,48,1500]{2,1,0:T(8,128)(2,1)S(1)}, bf16[4,48,1500]{2,1,0:T(8,128)(2,1)S(1)}, u32[]{:S(2)}, u32[]{:S(2)}) collective-permute-start(bf16[4,48,1500]{2,1,0:T(8,128)(2,1)S(1)} %slice.7), channel_id=1, source_target_pairs={{1,0},{2,1},{3,2},{4,3},{5,4},{6,5},{7,6},{8,7},{9,8},{10,9},{11,1... | collective-permute-start | bytes 1728008 | tf_op jit(solution)/shard_map/ppermute | solution.py:314
  2.5 1.7 %copy-done = bf16[16,48,1500]{2,1,0:T(8,128)(2,1)S(1)} copy-done((bf16[16,48,1500]{2,1,0:T(8,128)(2,1)S(1)}, bf16[16,48,1500]{2,1,0:T(8,128)(2,1)}, u32[]{:S(2)}) %copy-start) | copy-done | bytes 2304024
  4.1 1.4 %copy-done.2 = bf16[1500,512]{1,0:T(8,128)(2,1)S(1)} copy-done((bf16[1500,512]{1,0:T(8,128)(2,1)S(1)}, bf16[1500,512]{1,0:T(8,128)(2,1)}, u32[]{:S(2)}) %copy-start.2) | copy-done | bytes 1536024
  6.2 3.3 %whiten.1 = (f32[4224,128]{1,0:T(8,128)S(1)}, f32[3,512,128]{2,1,0:T(8,128)S(1)}, s32[19]{0:T(128)S(1)}) custom-call(s32[1]{0:T(128)} %bitcast.me_ref, s32[64]{0:T(128)S(1)} %copy-done.5, bf16[16,48,1500]{2,1,0:T(8,128)(2,1)S(1)} %copy-done, bf16[1500,512]{1,0:T(8,128)(2,1)S(1)} %copy-done.2, bf16[256,256]{1,0:T(8,128)(2,1)S(1)} %copy-done.4), custom_call_target="tpu_custom_call" | custom-call | flops 960233472 | bytes 8388608 | tf_op jit(solution)/shard_map/whiten/pallas_call | solution.py:327
  9.5 2.5 %finish.1 = (f32[4224,128]{1,0:T(8,128)S(1)}, f32[3,512,128]{2,1,0:T(8,128)S(1)}, bf16[32,16,384]{2,1,0:T(8,128)(2,1)}, bf16[32,16,384]{2,1,0:T(8,128)(2,1)}) custom-call(s32[19]{0:T(128)S(1)} %get-tuple-element.41.slot_ref, bf16[16,48,1500]{2,1,0:T(8,128)(2,1)S(1)} %copy-done.1, ...), custom_call_target="tpu_custom_call", output_to_operand_aliasing={{0}: (5, {}), {1}: (6, {})} | custom-call | tf_op jit(solution)/shard_map/finish/pallas_call | solution.py:341
  12.0 10.3 %all-to-all-start.1 = ((bf16[32,16,384]{2,1,0:T(8,128)(2,1)}), bf16[32,16,384]{2,1,0:T(8,128)(2,1)S(1)}, u32[]{:S(2)}, u32[]{:S(2)}) async-start(bf16[32,16,384]{2,1,0:T(8,128)(2,1)} %get-tuple-element.46), calls=%async_computation.1 | async-start | bytes 786432 | tf_op jit(solution)/shard_map/all_to_all | solution.py:354
  24.8 10.7 %all-to-all-done.1.rows_ref = bf16[32,16,384]{2,1,0:T(8,128)(2,1)S(1)} async-done(((bf16[32,16,384]{2,1,0:T(8,128)(2,1)}), bf16[32,16,384]{2,1,0:T(8,128)(2,1)S(1)}, u32[]{:S(2)}, u32[]{:S(2)}) %all-to-all-start.1) | async-done | bytes 393248 | tf_op jit(solution)/shard_map/all_to_all | solution.py:354
  36.3 1.6 %collective-permute-start.4 = (bf16[4,96,128]{2,1,0:T(8,128)(2,1)S(1)}, bf16[4,96,128]{2,1,0:T(8,128)(2,1)S(1)}, u32[]{:S(2)}, u32[]{:S(2)}) collective-permute-start(bf16[4,96,128]{2,1,0:T(8,128)(2,1)S(1)} %get-tuple-element.77.refs_0_), channel_id=1, source_target_pairs={{0,8},{1,9},{2,10},{3,11},{4,12},{5,13},{6,14},{7,15},{8,0},{9,1},... | collective-permute-start | bytes 294920 | tf_op jit(solution)/shard_map/ppermute | solution.py:252
  37.9 0.8 %collective-permute-start.3 = (bf16[4,96,128]{2,1,0:T(8,128)(2,1)S(1)}, bf16[4,96,128]{2,1,0:T(8,128)(2,1)S(1)}, u32[]{:S(2)}, u32[]{:S(2)}) collective-permute-start(bf16[4,96,128]{2,1,0:T(8,128)(2,1)S(1)} %get-tuple-element.77.refs_0_), channel_id=1, source_target_pairs={{0,2},{1,3},{2,0},{3,1},{4,6},{5,7},{6,4},{7,5},{8,10},{9,11},{10,... | collective-permute-start | bytes 294920 | tf_op jit(solution)/shard_map/ppermute | solution.py:252
  38.7 1.5 %collective-permute-start.2 = (bf16[4,96,128]{2,1,0:T(8,128)(2,1)S(1)}, bf16[4,96,128]{2,1,0:T(8,128)(2,1)S(1)}, u32[]{:S(2)}, u32[]{:S(2)}) collective-permute-start(bf16[4,96,128]{2,1,0:T(8,128)(2,1)S(1)} %get-tuple-element.77.refs_0_), channel_id=1, source_target_pairs={{0,4},{1,5},{2,6},{3,7},{4,0},{5,1},{6,2},{7,3},{8,12},{9,13},{10,... | collective-permute-start | bytes 294920 | tf_op jit(solution)/shard_map/ppermute | solution.py:252
  40.2 1.2 %collective-permute-start.1 = (bf16[4,96,128]{2,1,0:T(8,128)(2,1)S(1)}, bf16[4,96,128]{2,1,0:T(8,128)(2,1)S(1)}, u32[]{:S(2)}, u32[]{:S(2)}) collective-permute-start(bf16[4,96,128]{2,1,0:T(8,128)(2,1)S(1)} %get-tuple-element.77.refs_0_), channel_id=1, source_target_pairs={{0,6},{1,7},{2,4},{3,5},{4,2},{5,3},{6,0},{7,1},{8,14},{9,15},{10,... | collective-permute-start | bytes 294920 | tf_op jit(solution)/shard_map/ppermute | solution.py:252
  41.4 2.1 %collective-permute-done.5.refs_5_ = bf16[4,96,128]{2,1,0:T(8,128)(2,1)S(1)} collective-permute-done((bf16[4,96,128]{2,1,0:T(8,128)(2,1)S(1)}, bf16[4,96,128]{2,1,0:T(8,128)(2,1)S(1)}, u32[]{:S(2)}, u32[]{:S(2)}) %collective-permute-start.5) | collective-permute-done | bytes 98336 | tf_op jit(solution)/shard_map/ppermute | solution.py:252
  43.6 0.8 %collective-permute-done.2.refs_2_ = bf16[4,96,128]{2,1,0:T(8,128)(2,1)S(1)} collective-permute-done((bf16[4,96,128]{2,1,0:T(8,128)(2,1)S(1)}, bf16[4,96,128]{2,1,0:T(8,128)(2,1)S(1)}, u32[]{:S(2)}, u32[]{:S(2)}) %collective-permute-start.2) | collective-permute-done | bytes 98336 | tf_op jit(solution)/shard_map/ppermute | solution.py:252
  44.4 1.3 %collective-permute-done.1.refs_1_ = bf16[4,96,128]{2,1,0:T(8,128)(2,1)S(1)} collective-permute-done((bf16[4,96,128]{2,1,0:T(8,128)(2,1)S(1)}, bf16[4,96,128]{2,1,0:T(8,128)(2,1)S(1)}, u32[]{:S(2)}, u32[]{:S(2)}) %collective-permute-start.1) | collective-permute-done | bytes 98336 | tf_op jit(solution)/shard_map/ppermute | solution.py:252
  46.4 1.2 %collective-permute-start.7 = (bf16[8,96,128]{2,1,0:T(8,128)(2,1)S(1)}, bf16[8,96,128]{2,1,0:T(8,128)(2,1)S(1)}, u32[]{:S(2)}, u32[]{:S(2)}) collective-permute-start(bf16[8,96,128]{2,1,0:T(8,128)(2,1)S(1)} %get-tuple-element.74), channel_id=1, source_target_pairs={{0,4},{1,5},{2,6},{3,7},{4,0},{5,1},{6,2},{7,3},{8,12},{9,13},{10,... | collective-permute-start | bytes 589832 | tf_op jit(solution)/shard_map/ppermute | solution.py:252
  48.4 2.7 %collective-permute-start.8 = (bf16[4,96,128]{2,1,0:T(8,128)(2,1)S(1)}, bf16[4,96,128]{2,1,0:T(8,128)(2,1)S(1)}, u32[]{:S(2)}, u32[]{:S(2)}) collective-permute-start(bf16[4,96,128]{2,1,0:T(8,128)(2,1)S(1)} %collective-permute-done.1.refs_1_), channel_id=1, source_target_pairs={{0,16},{1,17},{2,18},{3,19},{4,20},{5,21},{6,22},{7,23},{8,24},{9,... | collective-permute-start | bytes 294920 | tf_op jit(solution)/shard_map/ppermute | solution.py:252
  51.1 2.0 %left.1.left_ref = bf16[128,64,128]{2,1,0:T(8,128)(2,1)S(1)} custom-call(f32[4224,128]{1,0:T(8,128)S(1)} %get-tuple-element.49.turned_ref), custom_call_target="tpu_custom_call" | custom-call | flops 10000000 | bytes 8388608 | tf_op jit(solution)/shard_map/left/pallas_call | solution.py:372
  53.4 1.6 %collective-permute-done.8.refs_3_ = bf16[4,96,128]{2,1,0:T(8,128)(2,1)S(1)} collective-permute-done((bf16[4,96,128]{2,1,0:T(8,128)(2,1)S(1)}, bf16[4,96,128]{2,1,0:T(8,128)(2,1)S(1)}, u32[]{:S(2)}, u32[]{:S(2)}) %collective-permute-start.8) | collective-permute-done | bytes 98336 | tf_op jit(solution)/shard_map/ppermute | solution.py:252
  55.8 1.2 %collective-permute-start.13 = (bf16[4,96,128]{2,1,0:T(8,128)(2,1)S(1)}, bf16[4,96,128]{2,1,0:T(8,128)(2,1)S(1)}, u32[]{:S(2)}, u32[]{:S(2)}) collective-permute-start(bf16[4,96,128]{2,1,0:T(8,128)(2,1)S(1)} %slice.8), channel_id=1, source_target_pairs={{0,4},{1,5},{2,6},{3,7},{4,0},{5,1},{6,2},{7,3},{8,12},{9,13},{10,... | collective-permute-start | bytes 294920 | tf_op jit(solution)/shard_map/ppermute | solution.py:252
  56.9 1.1 %collective-permute-start.12 = (bf16[4,96,128]{2,1,0:T(8,128)(2,1)S(1)}, bf16[4,96,128]{2,1,0:T(8,128)(2,1)S(1)}, u32[]{:S(2)}, u32[]{:S(2)}) collective-permute-start(bf16[4,96,128]{2,1,0:T(8,128)(2,1)S(1)} %slice.8), channel_id=1, source_target_pairs={{0,2},{1,3},{2,0},{3,1},{4,6},{5,7},{6,4},{7,5},{8,10},{9,11},{10,... | collective-permute-start | bytes 294920 | tf_op jit(solution)/shard_map/ppermute | solution.py:252
  58.3 2.1 %collective-permute-done.10.refs_4_ = bf16[4,96,128]{2,1,0:T(8,128)(2,1)S(1)} collective-permute-done((bf16[4,96,128]{2,1,0:T(8,128)(2,1)S(1)}, bf16[4,96,128]{2,1,0:T(8,128)(2,1)S(1)}, u32[]{:S(2)}, u32[]{:S(2)}) %collective-permute-start.10) | collective-permute-done | bytes 98336 | tf_op jit(solution)/shard_map/ppermute | solution.py:252
  60.7 0.8 %collective-permute-done.12.refs_2_ = bf16[4,96,128]{2,1,0:T(8,128)(2,1)S(1)} collective-permute-done((bf16[4,96,128]{2,1,0:T(8,128)(2,1)S(1)}, bf16[4,96,128]{2,1,0:T(8,128)(2,1)S(1)}, u32[]{:S(2)}, u32[]{:S(2)}) %collective-permute-start.12) | collective-permute-done | bytes 98336 | tf_op jit(solution)/shard_map/ppermute | solution.py:252
  63.0 1.9 %correlate.1 = (f32[2,64,16,256]{3,2,1,0:T(8,128)}, f32[4352,128]{1,0:T(8,128)S(1)}) custom-call(s32[1]{0:T(128)} %bitcast.me_ref, bf16[128,64,128]{2,1,0:T(8,128)(2,1)S(1)} %left.1.left_ref, f32[4352,128]{1,0:T(8,128)S(1)} %products.5._, bf16[4,96,128]{2,1,0:T(8,128)(2,1)S(1)} %collective-permute-done.14.refs_0_, ...), custom_call_target="tpu_custom_call", output_to_operand_aliasing={{1}: (2, {})} | custom-call | tf_op jit(solution)/shard_map/correlate/pallas_call | solution.py:408
  (63 shorter events, 7.7 us)
Async XLA Ops:
  0.0 2.4 %copy-start.4 = (bf16[256,256]{1,0:T(8,128)(2,1)S(1)}, bf16[256,256]{1,0:T(8,128)(2,1)}, u32[]{:S(2)}) copy-start(bf16[256,256]{1,0:T(8,128)(2,1)} %constant.45.clone.band_ref) | copy-start | bytes 393220
  1.1 8.3 %collective-permute-start = (bf16[4,48,1500]{2,1,0:T(8,128)(2,1)S(1)}, bf16[4,48,1500]{2,1,0:T(8,128)(2,1)S(1)}, u32[]{:S(2)}, u32[]{:S(2)}) collective-permute-start(bf16[4,48,1500]{2,1,0:T(8,128)(2,1)S(1)} %slice.7), channel_id=1, source_target_pairs={{1,0},{2,1},{3,2},{4,3},{5,4},{6,5},{7,6},{8,7},{9,8},{10,9},{11,1... | collective-permute-start | bytes 1728008 | tf_op jit(solution)/shard_map/ppermute | solution.py:314
  2.5 1.7 %copy-start = (bf16[16,48,1500]{2,1,0:T(8,128)(2,1)S(1)}, bf16[16,48,1500]{2,1,0:T(8,128)(2,1)}, u32[]{:S(2)}) copy-start(bf16[16,48,1500]{2,1,0:T(8,128)(2,1)} %traces_ref.3) | copy-start | bytes 6912004
  4.1 1.4 %copy-start.2 = (bf16[1500,512]{1,0:T(8,128)(2,1)S(1)}, bf16[1500,512]{1,0:T(8,128)(2,1)}, u32[]{:S(2)}) copy-start(bf16[1500,512]{1,0:T(8,128)(2,1)} %constant.44.clone.table_ref) | copy-start | bytes 4608004
  6.2 3.3 %copy-start.1 = (bf16[16,48,1500]{2,1,0:T(8,128)(2,1)S(1)}, bf16[16,48,1500]{2,1,0:T(8,128)(2,1)}, u32[]{:S(2)}) copy-start(bf16[16,48,1500]{2,1,0:T(8,128)(2,1)} %traces_ref.3) | copy-start | bytes 6912004
  6.2 3.3 %copy-start.3 = (bf16[1500,512]{1,0:T(8,128)(2,1)S(1)}, bf16[1500,512]{1,0:T(8,128)(2,1)}, u32[]{:S(2)}) copy-start(bf16[1500,512]{1,0:T(8,128)(2,1)} %constant.44.clone.table_ref) | copy-start | bytes 4608004
  9.5 12.9 %copy-start.6 = (s32[64]{0:T(128)S(1)}, s32[64]{0:T(128)}, u32[]{:S(2)}) copy-start(s32[64]{0:T(128)} %index_ref.1) | copy-start | bytes 772
  12.0 23.5 %all-to-all-start.1 = ((bf16[32,16,384]{2,1,0:T(8,128)(2,1)}), bf16[32,16,384]{2,1,0:T(8,128)(2,1)S(1)}, u32[]{:S(2)}, u32[]{:S(2)}) async-start(bf16[32,16,384]{2,1,0:T(8,128)(2,1)} %get-tuple-element.46), calls=%async_computation.1 | async-start | bytes 786432 | tf_op jit(solution)/shard_map/all_to_all | solution.py:354
  36.2 7.4 %collective-permute-start.5 = (bf16[4,96,128]{2,1,0:T(8,128)(2,1)S(1)}, bf16[4,96,128]{2,1,0:T(8,128)(2,1)S(1)}, u32[]{:S(2)}, u32[]{:S(2)}) collective-permute-start(bf16[4,96,128]{2,1,0:T(8,128)(2,1)S(1)} %get-tuple-element.77.refs_0_), channel_id=1, source_target_pairs={{0,16},{1,17},{2,18},{3,19},{4,20},{5,21},{6,22},{7,23},{8,24},{9,... | collective-permute-start | bytes 294920 | tf_op jit(solution)/shard_map/ppermute | solution.py:252
  36.3 7.3 %collective-permute-start.4 = (bf16[4,96,128]{2,1,0:T(8,128)(2,1)S(1)}, bf16[4,96,128]{2,1,0:T(8,128)(2,1)S(1)}, u32[]{:S(2)}, u32[]{:S(2)}) collective-permute-start(bf16[4,96,128]{2,1,0:T(8,128)(2,1)S(1)} %get-tuple-element.77.refs_0_), channel_id=1, source_target_pairs={{0,8},{1,9},{2,10},{3,11},{4,12},{5,13},{6,14},{7,15},{8,0},{9,1},... | collective-permute-start | bytes 294920 | tf_op jit(solution)/shard_map/ppermute | solution.py:252
  37.9 5.7 %collective-permute-start.3 = (bf16[4,96,128]{2,1,0:T(8,128)(2,1)S(1)}, bf16[4,96,128]{2,1,0:T(8,128)(2,1)S(1)}, u32[]{:S(2)}, u32[]{:S(2)}) collective-permute-start(bf16[4,96,128]{2,1,0:T(8,128)(2,1)S(1)} %get-tuple-element.77.refs_0_), channel_id=1, source_target_pairs={{0,2},{1,3},{2,0},{3,1},{4,6},{5,7},{6,4},{7,5},{8,10},{9,11},{10,... | collective-permute-start | bytes 294920 | tf_op jit(solution)/shard_map/ppermute | solution.py:252
  38.7 5.6 %collective-permute-start.2 = (bf16[4,96,128]{2,1,0:T(8,128)(2,1)S(1)}, bf16[4,96,128]{2,1,0:T(8,128)(2,1)S(1)}, u32[]{:S(2)}, u32[]{:S(2)}) collective-permute-start(bf16[4,96,128]{2,1,0:T(8,128)(2,1)S(1)} %get-tuple-element.77.refs_0_), channel_id=1, source_target_pairs={{0,4},{1,5},{2,6},{3,7},{4,0},{5,1},{6,2},{7,3},{8,12},{9,13},{10,... | collective-permute-start | bytes 294920 | tf_op jit(solution)/shard_map/ppermute | solution.py:252
  40.2 5.5 %collective-permute-start.1 = (bf16[4,96,128]{2,1,0:T(8,128)(2,1)S(1)}, bf16[4,96,128]{2,1,0:T(8,128)(2,1)S(1)}, u32[]{:S(2)}, u32[]{:S(2)}) collective-permute-start(bf16[4,96,128]{2,1,0:T(8,128)(2,1)S(1)} %get-tuple-element.77.refs_0_), channel_id=1, source_target_pairs={{0,6},{1,7},{2,4},{3,5},{4,2},{5,3},{6,0},{7,1},{8,14},{9,15},{10,... | collective-permute-start | bytes 294920 | tf_op jit(solution)/shard_map/ppermute | solution.py:252
  45.7 9.2 %collective-permute-start.9 = (bf16[8,96,128]{2,1,0:T(8,128)(2,1)S(1)}, bf16[8,96,128]{2,1,0:T(8,128)(2,1)S(1)}, u32[]{:S(2)}, u32[]{:S(2)}) collective-permute-start(bf16[8,96,128]{2,1,0:T(8,128)(2,1)S(1)} %pad_maximum_fusion), channel_id=1, source_target_pairs={{0,8},{1,9},{2,10},{3,11},{4,12},{5,13},{6,14},{7,15},{8,0},{9,1},... | collective-permute-start | bytes 589832 | tf_op jit(solution)/shard_map/ppermute | solution.py:252
  46.4 8.6 %collective-permute-start.7 = (bf16[8,96,128]{2,1,0:T(8,128)(2,1)S(1)}, bf16[8,96,128]{2,1,0:T(8,128)(2,1)S(1)}, u32[]{:S(2)}, u32[]{:S(2)}) collective-permute-start(bf16[8,96,128]{2,1,0:T(8,128)(2,1)S(1)} %get-tuple-element.74), channel_id=1, source_target_pairs={{0,4},{1,5},{2,6},{3,7},{4,0},{5,1},{6,2},{7,3},{8,12},{9,13},{10,... | collective-permute-start | bytes 589832 | tf_op jit(solution)/shard_map/ppermute | solution.py:252
  47.6 7.3 %collective-permute-start.6 = (bf16[8,96,128]{2,1,0:T(8,128)(2,1)S(1)}, bf16[8,96,128]{2,1,0:T(8,128)(2,1)S(1)}, u32[]{:S(2)}, u32[]{:S(2)}) collective-permute-start(bf16[8,96,128]{2,1,0:T(8,128)(2,1)S(1)} %get-tuple-element.74), channel_id=1, source_target_pairs={{0,2},{1,3},{2,0},{3,1},{4,6},{5,7},{6,4},{7,5},{8,10},{9,11},{10,... | collective-permute-start | bytes 589832 | tf_op jit(solution)/shard_map/ppermute | solution.py:252
  48.4 6.6 %collective-permute-start.8 = (bf16[4,96,128]{2,1,0:T(8,128)(2,1)S(1)}, bf16[4,96,128]{2,1,0:T(8,128)(2,1)S(1)}, u32[]{:S(2)}, u32[]{:S(2)}) collective-permute-start(bf16[4,96,128]{2,1,0:T(8,128)(2,1)S(1)} %collective-permute-done.1.refs_1_), channel_id=1, source_target_pairs={{0,16},{1,17},{2,18},{3,19},{4,20},{5,21},{6,22},{7,23},{8,24},{9,... | collective-permute-start | bytes 294920 | tf_op jit(solution)/shard_map/ppermute | solution.py:252
  55.1 6.9 %collective-permute-start.11 = (bf16[52,96,128]{2,1,0:T(8,128)(2,1)S(1)}, bf16[52,96,128]{2,1,0:T(8,128)(2,1)S(1)}, u32[]{:S(2)}, u32[]{:S(2)}) collective-permute-start(bf16[52,96,128]{2,1,0:T(8,128)(2,1)S(1)} %constant_dynamic-update-slice_fusion.2), channel_id=1, source_target_pairs={{0,1},{1,0},{2,3},{3,2},{4,5},{5,4},{6,7},{7,6},{8,9},{9,8},{10,11... | collective-permute-start | bytes 3833864 | tf_op jit(solution)/shard_map/ppermute | solution.py:252
  55.2 5.2 %collective-permute-start.10 = (bf16[4,96,128]{2,1,0:T(8,128)(2,1)S(1)}, bf16[4,96,128]{2,1,0:T(8,128)(2,1)S(1)}, u32[]{:S(2)}, u32[]{:S(2)}) collective-permute-start(bf16[4,96,128]{2,1,0:T(8,128)(2,1)S(1)} %collective-permute-done.8.refs_3_), channel_id=1, source_target_pairs={{0,8},{1,9},{2,10},{3,11},{4,12},{5,13},{6,14},{7,15},{8,0},{9,1},... | collective-permute-start | bytes 294920 | tf_op jit(solution)/shard_map/ppermute | solution.py:252
  55.8 4.9 %collective-permute-start.13 = (bf16[4,96,128]{2,1,0:T(8,128)(2,1)S(1)}, bf16[4,96,128]{2,1,0:T(8,128)(2,1)S(1)}, u32[]{:S(2)}, u32[]{:S(2)}) collective-permute-start(bf16[4,96,128]{2,1,0:T(8,128)(2,1)S(1)} %slice.8), channel_id=1, source_target_pairs={{0,4},{1,5},{2,6},{3,7},{4,0},{5,1},{6,2},{7,3},{8,12},{9,13},{10,... | collective-permute-start | bytes 294920 | tf_op jit(solution)/shard_map/ppermute | solution.py:252
  56.9 4.6 %collective-permute-start.12 = (bf16[4,96,128]{2,1,0:T(8,128)(2,1)S(1)}, bf16[4,96,128]{2,1,0:T(8,128)(2,1)S(1)}, u32[]{:S(2)}, u32[]{:S(2)}) collective-permute-start(bf16[4,96,128]{2,1,0:T(8,128)(2,1)S(1)} %slice.8), channel_id=1, source_target_pairs={{0,2},{1,3},{2,0},{3,1},{4,6},{5,7},{6,4},{7,5},{8,10},{9,11},{10,... | collective-permute-start | bytes 294920 | tf_op jit(solution)/shard_map/ppermute | solution.py:252
  60.7 1.9 %collective-permute-start.15 = (bf16[4,96,128]{2,1,0:T(8,128)(2,1)S(1)}, bf16[4,96,128]{2,1,0:T(8,128)(2,1)S(1)}, u32[]{:S(2)}, u32[]{:S(2)}) collective-permute-start(bf16[4,96,128]{2,1,0:T(8,128)(2,1)S(1)} %collective-permute-done.13.refs_3_), channel_id=1, source_target_pairs={{0,1},{1,0},{2,3},{3,2},{4,5},{5,4},{6,7},{7,6},{8,9},{9,8},{10,11... | collective-permute-start | bytes 294920 | tf_op jit(solution)/shard_map/ppermute | solution.py:252
  61.5 1.3 %collective-permute-start.14 = (bf16[4,96,128]{2,1,0:T(8,128)(2,1)S(1)}, bf16[4,96,128]{2,1,0:T(8,128)(2,1)S(1)}, u32[]{:S(2)}, u32[]{:S(2)}) collective-permute-start(bf16[4,96,128]{2,1,0:T(8,128)(2,1)S(1)} %collective-permute-done.12.refs_2_), channel_id=1, source_target_pairs={{0,1},{1,0},{2,3},{3,2},{4,5},{5,4},{6,7},{7,6},{8,9},{9,8},{10,11... | collective-permute-start | bytes 294920 | tf_op jit(solution)/shard_map/ppermute | solution.py:252
  61.5 1.5 %collective-permute-start.16 = (bf16[4,96,128]{2,1,0:T(8,128)(2,1)S(1)}, bf16[4,96,128]{2,1,0:T(8,128)(2,1)S(1)}, u32[]{:S(2)}, u32[]{:S(2)}) collective-permute-start(bf16[4,96,128]{2,1,0:T(8,128)(2,1)S(1)} %collective-permute-done.10.refs_4_), channel_id=1, source_target_pairs={{0,1},{1,0},{2,3},{3,2},{4,5},{5,4},{6,7},{7,6},{8,9},{9,8},{10,11... | collective-permute-start | bytes 294920 | tf_op jit(solution)/shard_map/ppermute | solution.py:252
  (1 other events, 0.7 us)

commit v3 on v2

--- a/solution.py
+++ b/solution.py
@@ -279,9 +279,9 @@
     arrays = after_products(*lists(mid)[0])
     mid = [keep(array, names) for array, (_, names) in zip(arrays, mid)]
     last = [
+        send(piece(zz ^ x ^ y), z),
         send(piece(z ^ zz), x),
         send(piece(z ^ zz), y),
-        send(piece(zz ^ x ^ y), z),
     ]
     theirs = send([name for pair in near + mid for name in pair[1]], core)
     multiply(*lists(mid))

time: 65.2 us -> 65.2 us (level)
  no operation moved by 1% of the time
where the time goes in v3:
time: 65.2 us; the launch traced here: 64.9 us
  starting transfers between devices  25.4 us (39%)
  waiting for transfers between devices  20.3 us (31%)
  Pallas kernels  11.4 us (17%)
  local copies, waits for them, and re-layouts  5.59 us (9%)
  other arithmetic  1.25 us (2%)
  between operations  0.96 us (1%)
    ppermute x16, starting transfers between devices, send(): lax.ppermute(pack(names), 'chan', route)  13.7 us
    all_to_all x1, waiting for transfers between devices, exchange(): rows = lax.all_to_all(rows, 'chan', 0, 0, tiled=True)  10.7 us
    all_to_all x1, starting transfers between devices, exchange(): rows = lax.all_to_all(rows, 'chan', 0, 0, tiled=True)  10.5 us
    ppermute x16, waiting for transfers between devices, send(): lax.ppermute(pack(names), 'chan', route)  9.56 us
    unnamed x23, local copies, waits for them, and re-layouts  3.93 us
    pallas_call x1, Pallas kernels, per_device(): pl.pallas_call(functools.partial(whiten_kernel, chans, slots), in_specs=[...  3.3 us
    pallas_call x1, Pallas kernels, per_device(): pl.pallas_call(functools.partial(finish_kernel, chans, slots), in_specs=[...  2.46 us
    pallas_call x1, Pallas kernels, per_device(): pl.pallas_call(functools.partial(left_kernel, chans, depth), in_specs=[vm...  1.97 us
  transfers between devices with their start and end apart: 18, of which 11 were waited for; matrix products, arithmetic and copies ran while one was open for 3% of the time, Pallas kernels for 10%

profile of v3, /device:TPU:0, one launch (start us, length us, event | category | flops | bytes accessed | tf_op | source)
XLA Modules:
  0.0 64.9 jit_solution(4876518174844477017)
XLA Ops:
  0.0 1.1 %slice.7 = bf16[4,48,1500]{2,1,0:T(8,128)(2,1)S(1)} slice(bf16[16,48,1500]{2,1,0:T(8,128)(2,1)} %traces_ref.3), slice={[0:4], [0:48], [0:1500]} | slice | bytes 1152000 | tf_op jit(solution)/shard_map/slice | solution.py:314
  1.1 1.3 %collective-permute-start = (bf16[4,48,1500]{2,1,0:T(8,128)(2,1)S(1)}, bf16[4,48,1500]{2,1,0:T(8,128)(2,1)S(1)}, u32[]{:S(2)}, u32[]{:S(2)}) collective-permute-start(bf16[4,48,1500]{2,1,0:T(8,128)(2,1)S(1)} %slice.7), channel_id=1, source_target_pairs={{1,0},{2,1},{3,2},{4,3},{5,4},{6,5},{7,6},{8,7},{9,8},{10,9},{11,1... | collective-permute-start | bytes 1728008 | tf_op jit(solution)/shard_map/ppermute | solution.py:314
  2.5 1.7 %copy-done = bf16[16,48,1500]{2,1,0:T(8,128)(2,1)S(1)} copy-done((bf16[16,48,1500]{2,1,0:T(8,128)(2,1)S(1)}, bf16[16,48,1500]{2,1,0:T(8,128)(2,1)}, u32[]{:S(2)}) %copy-start) | copy-done | bytes 2304024
  4.1 1.4 %copy-done.2 = bf16[1500,512]{1,0:T(8,128)(2,1)S(1)} copy-done((bf16[1500,512]{1,0:T(8,128)(2,1)S(1)}, bf16[1500,512]{1,0:T(8,128)(2,1)}, u32[]{:S(2)}) %copy-start.2) | copy-done | bytes 1536024
  6.2 3.3 %whiten.1 = (f32[4224,128]{1,0:T(8,128)S(1)}, f32[3,512,128]{2,1,0:T(8,128)S(1)}, s32[19]{0:T(128)S(1)}) custom-call(s32[1]{0:T(128)} %bitcast.me_ref, s32[64]{0:T(128)S(1)} %copy-done.5, bf16[16,48,1500]{2,1,0:T(8,128)(2,1)S(1)} %copy-done, bf16[1500,512]{1,0:T(8,128)(2,1)S(1)} %copy-done.2, bf16[256,256]{1,0:T(8,128)(2,1)S(1)} %copy-done.4), custom_call_target="tpu_custom_call" | custom-call | flops 960233472 | bytes 8388608 | tf_op jit(solution)/shard_map/whiten/pallas_call | solution.py:327
  9.5 2.5 %finish.1 = (f32[4224,128]{1,0:T(8,128)S(1)}, f32[3,512,128]{2,1,0:T(8,128)S(1)}, bf16[32,16,384]{2,1,0:T(8,128)(2,1)}, bf16[32,16,384]{2,1,0:T(8,128)(2,1)}) custom-call(s32[19]{0:T(128)S(1)} %get-tuple-element.41.slot_ref, bf16[16,48,1500]{2,1,0:T(8,128)(2,1)S(1)} %copy-done.1, ...), custom_call_target="tpu_custom_call", output_to_operand_aliasing={{0}: (5, {}), {1}: (6, {})} | custom-call | tf_op jit(solution)/shard_map/finish/pallas_call | solution.py:341
  12.0 10.5 %all-to-all-start.1 = ((bf16[32,16,384]{2,1,0:T(8,128)(2,1)}), bf16[32,16,384]{2,1,0:T(8,128)(2,1)S(1)}, u32[]{:S(2)}, u32[]{:S(2)}) async-start(bf16[32,16,384]{2,1,0:T(8,128)(2,1)} %get-tuple-element.46), calls=%async_computation.1 | async-start | bytes 786432 | tf_op jit(solution)/shard_map/all_to_all | solution.py:354
  24.9 10.7 %all-to-all-done.1.rows_ref = bf16[32,16,384]{2,1,0:T(8,128)(2,1)S(1)} async-done(((bf16[32,16,384]{2,1,0:T(8,128)(2,1)}), bf16[32,16,384]{2,1,0:T(8,128)(2,1)S(1)}, u32[]{:S(2)}, u32[]{:S(2)}) %all-to-all-start.1) | async-done | bytes 393248 | tf_op jit(solution)/shard_map/all_to_all | solution.py:354
  36.4 1.6 %collective-permute-start.4 = (bf16[4,96,128]{2,1,0:T(8,128)(2,1)S(1)}, bf16[4,96,128]{2,1,0:T(8,128)(2,1)S(1)}, u32[]{:S(2)}, u32[]{:S(2)}) collective-permute-start(bf16[4,96,128]{2,1,0:T(8,128)(2,1)S(1)} %get-tuple-element.77.refs_0_), channel_id=1, source_target_pairs={{0,8},{1,9},{2,10},{3,11},{4,12},{5,13},{6,14},{7,15},{8,0},{9,1},... | collective-permute-start | bytes 294920 | tf_op jit(solution)/shard_map/ppermute | solution.py:252
  38.0 0.8 %collective-permute-start.3 = (bf16[4,96,128]{2,1,0:T(8,128)(2,1)S(1)}, bf16[4,96,128]{2,1,0:T(8,128)(2,1)S(1)}, u32[]{:S(2)}, u32[]{:S(2)}) collective-permute-start(bf16[4,96,128]{2,1,0:T(8,128)(2,1)S(1)} %get-tuple-element.77.refs_0_), channel_id=1, source_target_pairs={{0,2},{1,3},{2,0},{3,1},{4,6},{5,7},{6,4},{7,5},{8,10},{9,11},{10,... | collective-permute-start | bytes 294920 | tf_op jit(solution)/shard_map/ppermute | solution.py:252
  38.9 1.5 %collective-permute-start.2 = (bf16[4,96,128]{2,1,0:T(8,128)(2,1)S(1)}, bf16[4,96,128]{2,1,0:T(8,128)(2,1)S(1)}, u32[]{:S(2)}, u32[]{:S(2)}) collective-permute-start(bf16[4,96,128]{2,1,0:T(8,128)(2,1)S(1)} %get-tuple-element.77.refs_0_), channel_id=1, source_target_pairs={{0,4},{1,5},{2,6},{3,7},{4,0},{5,1},{6,2},{7,3},{8,12},{9,13},{10,... | collective-permute-start | bytes 294920 | tf_op jit(solution)/shard_map/ppermute | solution.py:252
  40.3 1.2 %collective-permute-start.1 = (bf16[4,96,128]{2,1,0:T(8,128)(2,1)S(1)}, bf16[4,96,128]{2,1,0:T(8,128)(2,1)S(1)}, u32[]{:S(2)}, u32[]{:S(2)}) collective-permute-start(bf16[4,96,128]{2,1,0:T(8,128)(2,1)S(1)} %get-tuple-element.77.refs_0_), channel_id=1, source_target_pairs={{0,6},{1,7},{2,4},{3,5},{4,2},{5,3},{6,0},{7,1},{8,14},{9,15},{10,... | collective-permute-start | bytes 294920 | tf_op jit(solution)/shard_map/ppermute | solution.py:252
  41.5 2.1 %collective-permute-done.5.refs_5_ = bf16[4,96,128]{2,1,0:T(8,128)(2,1)S(1)} collective-permute-done((bf16[4,96,128]{2,1,0:T(8,128)(2,1)S(1)}, bf16[4,96,128]{2,1,0:T(8,128)(2,1)S(1)}, u32[]{:S(2)}, u32[]{:S(2)}) %collective-permute-start.5) | collective-permute-done | bytes 98336 | tf_op jit(solution)/shard_map/ppermute | solution.py:252
  43.7 0.8 %collective-permute-done.2.refs_2_ = bf16[4,96,128]{2,1,0:T(8,128)(2,1)S(1)} collective-permute-done((bf16[4,96,128]{2,1,0:T(8,128)(2,1)S(1)}, bf16[4,96,128]{2,1,0:T(8,128)(2,1)S(1)}, u32[]{:S(2)}, u32[]{:S(2)}) %collective-permute-start.2) | collective-permute-done | bytes 98336 | tf_op jit(solution)/shard_map/ppermute | solution.py:252
  44.5 1.3 %collective-permute-done.1.refs_1_ = bf16[4,96,128]{2,1,0:T(8,128)(2,1)S(1)} collective-permute-done((bf16[4,96,128]{2,1,0:T(8,128)(2,1)S(1)}, bf16[4,96,128]{2,1,0:T(8,128)(2,1)S(1)}, u32[]{:S(2)}, u32[]{:S(2)}) %collective-permute-start.1) | collective-permute-done | bytes 98336 | tf_op jit(solution)/shard_map/ppermute | solution.py:252
  46.5 1.2 %collective-permute-start.7 = (bf16[8,96,128]{2,1,0:T(8,128)(2,1)S(1)}, bf16[8,96,128]{2,1,0:T(8,128)(2,1)S(1)}, u32[]{:S(2)}, u32[]{:S(2)}) collective-permute-start(bf16[8,96,128]{2,1,0:T(8,128)(2,1)S(1)} %get-tuple-element.74), channel_id=1, source_target_pairs={{0,4},{1,5},{2,6},{3,7},{4,0},{5,1},{6,2},{7,3},{8,12},{9,13},{10,... | collective-permute-start | bytes 589832 | tf_op jit(solution)/shard_map/ppermute | solution.py:252
  48.5 2.7 %collective-permute-start.8 = (bf16[4,96,128]{2,1,0:T(8,128)(2,1)S(1)}, bf16[4,96,128]{2,1,0:T(8,128)(2,1)S(1)}, u32[]{:S(2)}, u32[]{:S(2)}) collective-permute-start(bf16[4,96,128]{2,1,0:T(8,128)(2,1)S(1)} %collective-permute-done.1.refs_1_), channel_id=1, source_target_pairs={{0,16},{1,17},{2,18},{3,19},{4,20},{5,21},{6,22},{7,23},{8,24},{9,... | collective-permute-start | bytes 294920 | tf_op jit(solution)/shard_map/ppermute | solution.py:252
  51.2 2.0 %left.1.left_ref = bf16[128,64,128]{2,1,0:T(8,128)(2,1)S(1)} custom-call(f32[4224,128]{1,0:T(8,128)S(1)} %get-tuple-element.49.turned_ref), custom_call_target="tpu_custom_call" | custom-call | flops 10000000 | bytes 8388608 | tf_op jit(solution)/shard_map/left/pallas_call | solution.py:372
  53.5 1.6 %collective-permute-done.8.refs_3_ = bf16[4,96,128]{2,1,0:T(8,128)(2,1)S(1)} collective-permute-done((bf16[4,96,128]{2,1,0:T(8,128)(2,1)S(1)}, bf16[4,96,128]{2,1,0:T(8,128)(2,1)S(1)}, u32[]{:S(2)}, u32[]{:S(2)}) %collective-permute-start.8) | collective-permute-done | bytes 98336 | tf_op jit(solution)/shard_map/ppermute | solution.py:252
  55.3 1.3 %collective-permute-start.10 = (bf16[4,96,128]{2,1,0:T(8,128)(2,1)S(1)}, bf16[4,96,128]{2,1,0:T(8,128)(2,1)S(1)}, u32[]{:S(2)}, u32[]{:S(2)}) collective-permute-start(bf16[4,96,128]{2,1,0:T(8,128)(2,1)S(1)} %slice.8), channel_id=1, source_target_pairs={{0,4},{1,5},{2,6},{3,7},{4,0},{5,1},{6,2},{7,3},{8,12},{9,13},{10,... | collective-permute-start | bytes 294920 | tf_op jit(solution)/shard_map/ppermute | solution.py:252
  56.7 1.3 %collective-permute-start.12 = (bf16[4,96,128]{2,1,0:T(8,128)(2,1)S(1)}, bf16[4,96,128]{2,1,0:T(8,128)(2,1)S(1)}, u32[]{:S(2)}, u32[]{:S(2)}) collective-permute-start(bf16[4,96,128]{2,1,0:T(8,128)(2,1)S(1)} %collective-permute-done.8.refs_3_), channel_id=1, source_target_pairs={{0,8},{1,9},{2,10},{3,11},{4,12},{5,13},{6,14},{7,15},{8,0},{9,1},... | collective-permute-start | bytes 294920 | tf_op jit(solution)/shard_map/ppermute | solution.py:252
  58.4 2.2 %collective-permute-done.10.refs_4_ = bf16[4,96,128]{2,1,0:T(8,128)(2,1)S(1)} collective-permute-done((bf16[4,96,128]{2,1,0:T(8,128)(2,1)S(1)}, bf16[4,96,128]{2,1,0:T(8,128)(2,1)S(1)}, u32[]{:S(2)}, u32[]{:S(2)}) %collective-permute-start.10) | collective-permute-done | bytes 98336 | tf_op jit(solution)/shard_map/ppermute | solution.py:252
  60.6 1.0 %collective-permute-done.13.refs_3_ = bf16[4,96,128]{2,1,0:T(8,128)(2,1)S(1)} collective-permute-done((bf16[4,96,128]{2,1,0:T(8,128)(2,1)S(1)}, bf16[4,96,128]{2,1,0:T(8,128)(2,1)S(1)}, u32[]{:S(2)}, u32[]{:S(2)}) %collective-permute-start.13) | collective-permute-done | bytes 98336 | tf_op jit(solution)/shard_map/ppermute | solution.py:252
  63.0 1.9 %correlate.1 = (f32[2,64,16,256]{3,2,1,0:T(8,128)}, f32[4352,128]{1,0:T(8,128)S(1)}) custom-call(s32[1]{0:T(128)} %bitcast.me_ref, bf16[128,64,128]{2,1,0:T(8,128)(2,1)S(1)} %left.1.left_ref, f32[4352,128]{1,0:T(8,128)S(1)} %products.5._, bf16[4,96,128]{2,1,0:T(8,128)(2,1)S(1)} %collective-permute-done.14.refs_0_, ...), custom_call_target="tpu_custom_call", output_to_operand_aliasing={{1}: (2, {})} | custom-call | tf_op jit(solution)/shard_map/correlate/pallas_call | solution.py:408
  (63 shorter events, 7.0 us)
Async XLA Ops:
  0.0 2.4 %copy-start.4 = (bf16[256,256]{1,0:T(8,128)(2,1)S(1)}, bf16[256,256]{1,0:T(8,128)(2,1)}, u32[]{:S(2)}) copy-start(bf16[256,256]{1,0:T(8,128)(2,1)} %constant.45.clone.band_ref) | copy-start | bytes 393220
  1.1 8.3 %collective-permute-start = (bf16[4,48,1500]{2,1,0:T(8,128)(2,1)S(1)}, bf16[4,48,1500]{2,1,0:T(8,128)(2,1)S(1)}, u32[]{:S(2)}, u32[]{:S(2)}) collective-permute-start(bf16[4,48,1500]{2,1,0:T(8,128)(2,1)S(1)} %slice.7), channel_id=1, source_target_pairs={{1,0},{2,1},{3,2},{4,3},{5,4},{6,5},{7,6},{8,7},{9,8},{10,9},{11,1... | collective-permute-start | bytes 1728008 | tf_op jit(solution)/shard_map/ppermute | solution.py:314
  2.5 1.7 %copy-start = (bf16[16,48,1500]{2,1,0:T(8,128)(2,1)S(1)}, bf16[16,48,1500]{2,1,0:T(8,128)(2,1)}, u32[]{:S(2)}) copy-start(bf16[16,48,1500]{2,1,0:T(8,128)(2,1)} %traces_ref.3) | copy-start | bytes 6912004
  4.1 1.4 %copy-start.2 = (bf16[1500,512]{1,0:T(8,128)(2,1)S(1)}, bf16[1500,512]{1,0:T(8,128)(2,1)}, u32[]{:S(2)}) copy-start(bf16[1500,512]{1,0:T(8,128)(2,1)} %constant.44.clone.table_ref) | copy-start | bytes 4608004
  6.2 3.3 %copy-start.1 = (bf16[16,48,1500]{2,1,0:T(8,128)(2,1)S(1)}, bf16[16,48,1500]{2,1,0:T(8,128)(2,1)}, u32[]{:S(2)}) copy-start(bf16[16,48,1500]{2,1,0:T(8,128)(2,1)} %traces_ref.3) | copy-start | bytes 6912004
  6.2 3.3 %copy-start.3 = (bf16[1500,512]{1,0:T(8,128)(2,1)S(1)}, bf16[1500,512]{1,0:T(8,128)(2,1)}, u32[]{:S(2)}) copy-start(bf16[1500,512]{1,0:T(8,128)(2,1)} %constant.44.clone.table_ref) | copy-start | bytes 4608004
  9.5 13.0 %copy-start.6 = (s32[64]{0:T(128)S(1)}, s32[64]{0:T(128)}, u32[]{:S(2)}) copy-start(s32[64]{0:T(128)} %index_ref.1) | copy-start | bytes 772
  12.0 23.6 %all-to-all-start.1 = ((bf16[32,16,384]{2,1,0:T(8,128)(2,1)}), bf16[32,16,384]{2,1,0:T(8,128)(2,1)S(1)}, u32[]{:S(2)}, u32[]{:S(2)}) async-start(bf16[32,16,384]{2,1,0:T(8,128)(2,1)} %get-tuple-element.46), calls=%async_computation.1 | async-start | bytes 786432 | tf_op jit(solution)/shard_map/all_to_all | solution.py:354
  36.3 7.4 %collective-permute-start.5 = (bf16[4,96,128]{2,1,0:T(8,128)(2,1)S(1)}, bf16[4,96,128]{2,1,0:T(8,128)(2,1)S(1)}, u32[]{:S(2)}, u32[]{:S(2)}) collective-permute-start(bf16[4,96,128]{2,1,0:T(8,128)(2,1)S(1)} %get-tuple-element.77.refs_0_), channel_id=1, source_target_pairs={{0,16},{1,17},{2,18},{3,19},{4,20},{5,21},{6,22},{7,23},{8,24},{9,... | collective-permute-start | bytes 294920 | tf_op jit(solution)/shard_map/ppermute | solution.py:252
  36.4 7.3 %collective-permute-start.4 = (bf16[4,96,128]{2,1,0:T(8,128)(2,1)S(1)}, bf16[4,96,128]{2,1,0:T(8,128)(2,1)S(1)}, u32[]{:S(2)}, u32[]{:S(2)}) collective-permute-start(bf16[4,96,128]{2,1,0:T(8,128)(2,1)S(1)} %get-tuple-element.77.refs_0_), channel_id=1, source_target_pairs={{0,8},{1,9},{2,10},{3,11},{4,12},{5,13},{6,14},{7,15},{8,0},{9,1},... | collective-permute-start | bytes 294920 | tf_op jit(solution)/shard_map/ppermute | solution.py:252
  38.0 5.7 %collective-permute-start.3 = (bf16[4,96,128]{2,1,0:T(8,128)(2,1)S(1)}, bf16[4,96,128]{2,1,0:T(8,128)(2,1)S(1)}, u32[]{:S(2)}, u32[]{:S(2)}) collective-permute-start(bf16[4,96,128]{2,1,0:T(8,128)(2,1)S(1)} %get-tuple-element.77.refs_0_), channel_id=1, source_target_pairs={{0,2},{1,3},{2,0},{3,1},{4,6},{5,7},{6,4},{7,5},{8,10},{9,11},{10,... | collective-permute-start | bytes 294920 | tf_op jit(solution)/shard_map/ppermute | solution.py:252
  38.9 5.6 %collective-permute-start.2 = (bf16[4,96,128]{2,1,0:T(8,128)(2,1)S(1)}, bf16[4,96,128]{2,1,0:T(8,128)(2,1)S(1)}, u32[]{:S(2)}, u32[]{:S(2)}) collective-permute-start(bf16[4,96,128]{2,1,0:T(8,128)(2,1)S(1)} %get-tuple-element.77.refs_0_), channel_id=1, source_target_pairs={{0,4},{1,5},{2,6},{3,7},{4,0},{5,1},{6,2},{7,3},{8,12},{9,13},{10,... | collective-permute-start | bytes 294920 | tf_op jit(solution)/shard_map/ppermute | solution.py:252
  40.3 5.5 %collective-permute-start.1 = (bf16[4,96,128]{2,1,0:T(8,128)(2,1)S(1)}, bf16[4,96,128]{2,1,0:T(8,128)(2,1)S(1)}, u32[]{:S(2)}, u32[]{:S(2)}) collective-permute-start(bf16[4,96,128]{2,1,0:T(8,128)(2,1)S(1)} %get-tuple-element.77.refs_0_), channel_id=1, source_target_pairs={{0,6},{1,7},{2,4},{3,5},{4,2},{5,3},{6,0},{7,1},{8,14},{9,15},{10,... | collective-permute-start | bytes 294920 | tf_op jit(solution)/shard_map/ppermute | solution.py:252
  45.9 9.2 %collective-permute-start.9 = (bf16[8,96,128]{2,1,0:T(8,128)(2,1)S(1)}, bf16[8,96,128]{2,1,0:T(8,128)(2,1)S(1)}, u32[]{:S(2)}, u32[]{:S(2)}) collective-permute-start(bf16[8,96,128]{2,1,0:T(8,128)(2,1)S(1)} %pad_maximum_fusion), channel_id=1, source_target_pairs={{0,8},{1,9},{2,10},{3,11},{4,12},{5,13},{6,14},{7,15},{8,0},{9,1},... | collective-permute-start | bytes 589832 | tf_op jit(solution)/shard_map/ppermute | solution.py:252
  46.5 8.6 %collective-permute-start.7 = (bf16[8,96,128]{2,1,0:T(8,128)(2,1)S(1)}, bf16[8,96,128]{2,1,0:T(8,128)(2,1)S(1)}, u32[]{:S(2)}, u32[]{:S(2)}) collective-permute-start(bf16[8,96,128]{2,1,0:T(8,128)(2,1)S(1)} %get-tuple-element.74), channel_id=1, source_target_pairs={{0,4},{1,5},{2,6},{3,7},{4,0},{5,1},{6,2},{7,3},{8,12},{9,13},{10,... | collective-permute-start | bytes 589832 | tf_op jit(solution)/shard_map/ppermute | solution.py:252
  47.8 7.3 %collective-permute-start.6 = (bf16[8,96,128]{2,1,0:T(8,128)(2,1)S(1)}, bf16[8,96,128]{2,1,0:T(8,128)(2,1)S(1)}, u32[]{:S(2)}, u32[]{:S(2)}) collective-permute-start(bf16[8,96,128]{2,1,0:T(8,128)(2,1)S(1)} %get-tuple-element.74), channel_id=1, source_target_pairs={{0,2},{1,3},{2,0},{3,1},{4,6},{5,7},{6,4},{7,5},{8,10},{9,11},{10,... | collective-permute-start | bytes 589832 | tf_op jit(solution)/shard_map/ppermute | solution.py:252
  48.5 6.6 %collective-permute-start.8 = (bf16[4,96,128]{2,1,0:T(8,128)(2,1)S(1)}, bf16[4,96,128]{2,1,0:T(8,128)(2,1)S(1)}, u32[]{:S(2)}, u32[]{:S(2)}) collective-permute-start(bf16[4,96,128]{2,1,0:T(8,128)(2,1)S(1)} %collective-permute-done.1.refs_1_), channel_id=1, source_target_pairs={{0,16},{1,17},{2,18},{3,19},{4,20},{5,21},{6,22},{7,23},{8,24},{9,... | collective-permute-start | bytes 294920 | tf_op jit(solution)/shard_map/ppermute | solution.py:252
  55.2 6.9 %collective-permute-start.11 = (bf16[52,96,128]{2,1,0:T(8,128)(2,1)S(1)}, bf16[52,96,128]{2,1,0:T(8,128)(2,1)S(1)}, u32[]{:S(2)}, u32[]{:S(2)}) collective-permute-start(bf16[52,96,128]{2,1,0:T(8,128)(2,1)S(1)} %constant_dynamic-update-slice_fusion.2), channel_id=1, source_target_pairs={{0,1},{1,0},{2,3},{3,2},{4,5},{5,4},{6,7},{7,6},{8,9},{9,8},{10,11... | collective-permute-start | bytes 3833864 | tf_op jit(solution)/shard_map/ppermute | solution.py:252
  55.3 5.2 %collective-permute-start.10 = (bf16[4,96,128]{2,1,0:T(8,128)(2,1)S(1)}, bf16[4,96,128]{2,1,0:T(8,128)(2,1)S(1)}, u32[]{:S(2)}, u32[]{:S(2)}) collective-permute-start(bf16[4,96,128]{2,1,0:T(8,128)(2,1)S(1)} %slice.8), channel_id=1, source_target_pairs={{0,4},{1,5},{2,6},{3,7},{4,0},{5,1},{6,2},{7,3},{8,12},{9,13},{10,... | collective-permute-start | bytes 294920 | tf_op jit(solution)/shard_map/ppermute | solution.py:252
  56.7 4.9 %collective-permute-start.13 = (bf16[4,96,128]{2,1,0:T(8,128)(2,1)S(1)}, bf16[4,96,128]{2,1,0:T(8,128)(2,1)S(1)}, u32[]{:S(2)}, u32[]{:S(2)}) collective-permute-start(bf16[4,96,128]{2,1,0:T(8,128)(2,1)S(1)} %slice.8), channel_id=1, source_target_pairs={{0,2},{1,3},{2,0},{3,1},{4,6},{5,7},{6,4},{7,5},{8,10},{9,11},{10,... | collective-permute-start | bytes 294920 | tf_op jit(solution)/shard_map/ppermute | solution.py:252
  56.7 4.9 %collective-permute-start.12 = (bf16[4,96,128]{2,1,0:T(8,128)(2,1)S(1)}, bf16[4,96,128]{2,1,0:T(8,128)(2,1)S(1)}, u32[]{:S(2)}, u32[]{:S(2)}) collective-permute-start(bf16[4,96,128]{2,1,0:T(8,128)(2,1)S(1)} %collective-permute-done.8.refs_3_), channel_id=1, source_target_pairs={{0,8},{1,9},{2,10},{3,11},{4,12},{5,13},{6,14},{7,15},{8,0},{9,1},... | collective-permute-start | bytes 294920 | tf_op jit(solution)/shard_map/ppermute | solution.py:252
  60.6 2.3 %collective-permute-start.16 = (bf16[4,96,128]{2,1,0:T(8,128)(2,1)S(1)}, bf16[4,96,128]{2,1,0:T(8,128)(2,1)S(1)}, u32[]{:S(2)}, u32[]{:S(2)}) collective-permute-start(bf16[4,96,128]{2,1,0:T(8,128)(2,1)S(1)} %collective-permute-done.10.refs_4_), channel_id=1, source_target_pairs={{0,1},{1,0},{2,3},{3,2},{4,5},{5,4},{6,7},{7,6},{8,9},{9,8},{10,11... | collective-permute-start | bytes 294920 | tf_op jit(solution)/shard_map/ppermute | solution.py:252
  61.6 1.3 %collective-permute-start.15 = (bf16[4,96,128]{2,1,0:T(8,128)(2,1)S(1)}, bf16[4,96,128]{2,1,0:T(8,128)(2,1)S(1)}, u32[]{:S(2)}, u32[]{:S(2)}) collective-permute-start(bf16[4,96,128]{2,1,0:T(8,128)(2,1)S(1)} %collective-permute-done.13.refs_3_), channel_id=1, source_target_pairs={{0,1},{1,0},{2,3},{3,2},{4,5},{5,4},{6,7},{7,6},{8,9},{9,8},{10,11... | collective-permute-start | bytes 294920 | tf_op jit(solution)/shard_map/ppermute | solution.py:252
  61.6 1.4 %collective-permute-start.14 = (bf16[4,96,128]{2,1,0:T(8,128)(2,1)S(1)}, bf16[4,96,128]{2,1,0:T(8,128)(2,1)S(1)}, u32[]{:S(2)}, u32[]{:S(2)}) collective-permute-start(bf16[4,96,128]{2,1,0:T(8,128)(2,1)S(1)} %collective-permute-done.12.refs_2_), channel_id=1, source_target_pairs={{0,1},{1,0},{2,3},{3,2},{4,5},{5,4},{6,7},{7,6},{8,9},{9,8},{10,11... | collective-permute-start | bytes 294920 | tf_op jit(solution)/shard_map/ppermute | solution.py:252
  (1 other events, 0.7 us)
